TPU v7x, 128 devices: a whole 4x4x4 slice. The times are simulated.
128 devices in a mesh: gx: 8 (over z_lo, y), gy: 4 (over z_hi, core), gz: 4 (over x).
Axes of the slice: x: 4, y: 4, z: 4 (z_hi: 2, z_lo: 2; z = z_hi * 2 + z_lo), core: 2. Of those that a mesh axis runs over, the one named last changes fastest.
Arguments:
- positions: float32 [16, 4, 4, 3, 32], P('gx', 'gy', 'gz'), may hold values from 0 to 5, as said below
- counts: int32 [16, 4, 4], P('gx', 'gy', 'gz'), may hold values from 1 to 32, as said below
- scalars: bfloat16 [16, 4, 4, 32, 128], P('gx', 'gy', 'gz'), may hold values from -6 to 6
- vectors: bfloat16 [16, 4, 4, 32, 3, 128], P('gx', 'gy', 'gz'), may hold values from -6 to 6
- radial_in: bfloat16 [2, 8, 64], replicated, may hold values from -2 to 2
- radial_bias: float32 [2, 64], replicated, may hold values from -3 to 3
- radial_out: bfloat16 [2, 64, 512], replicated, may hold values from -0.75 to 0.75
- atom_in: bfloat16 [2, 128, 128], replicated, may hold values from -0.5 to 0.5
- atom_bias: float32 [2, 128], replicated, may hold values from -3 to 3
- atom_out: bfloat16 [2, 128, 512], replicated, may hold values from -0.5 to 0.5
- readout_in: bfloat16 [128, 64], replicated, may hold values from -0.5 to 0.5
- readout_out: float32 [64], replicated, may hold values from -0.75 to 0.75
Outputs:
- scalars_out: bfloat16 [16, 4, 4, 32, 128], P('gx', 'gy', 'gz')
- vectors_out: bfloat16 [16, 4, 4, 32, 3, 128], P('gx', 'gy', 'gz')
- energy: float32 [1], replicated
Inputs may be any that keep to these rules, and one draw needn't show every extreme that they name: `counts`: some cell of every draw holds 32 atoms and some other cell one atom. `positions`: the slots of a cell sit on distinct sites of a jittered lattice, so that any two slots, also of neighbouring cells, lie at least 0.5 apart.
All inputs are finite; a program needn't handle non-finite values.
Results may differ from a plain program's by a relative error of at most 0.0075.
Values may be sent and summed in bfloat16 or wider, within the bound.
No kernel may reach another device: no remote copies, remote signals or barrier semaphores. Data moves between devices by JAX's collectives and lax.ppermute only.
A program may use at most 64 MiB of HBM per device.

v0:
```python
import math

import jax
import jax.numpy as jnp
from jax import lax
from jax.sharding import PartitionSpec as P

cutoff = 5.0
message_scale = 0.5


def extended(block, sides, width):
    for axis, dim in sides:
        count = lax.axis_size(axis)
        forward = [(i, i + 1) for i in range(count - 1)]
        forward.append((count - 1, 0))
        backward = [(target, source) for source, target in forward]
        low = lax.ppermute(
            lax.slice_in_dim(block, block.shape[dim] - width, None, axis=dim), axis, forward
        )
        high = lax.ppermute(lax.slice_in_dim(block, 0, width, axis=dim), axis, backward)
        block = jnp.concatenate([low, block, high], axis=dim)
    return block


def offsets_table():
    index = lax.broadcasted_iota(jnp.int32, (27, 3), 0)
    column = lax.broadcasted_iota(jnp.int32, (27, 3), 1)
    digit = jnp.where(column == 0, index // 9, jnp.where(column == 1, index // 3 % 3, index % 3))
    return (digit - 1).astype(jnp.float32)


def atom_gates(states, atom_in, atom_bias, atom_out):
    lead = states.shape[:-1]
    width = states.shape[-1]
    flat = states.reshape(-1, width)
    hidden = jax.nn.silu(
        jnp.dot(flat, atom_in, preferred_element_type=jnp.float32) + atom_bias
    ).astype(jnp.bfloat16)
    gates = jnp.dot(hidden, atom_out, preferred_element_type=jnp.float32).astype(jnp.bfloat16)
    return gates.reshape(lead + (4, width))


def receiver_block(
    start,
    row_count,
    near_pos,
    near_live,
    own_pos,
    plain_side,
    gate_c,
    pair_g,
    radial_in,
    radial_bias,
    radial_out,
):
    slots = own_pos.shape[1]
    near_count = near_pos.shape[0]
    width = gate_c.shape[-1]
    mine = lax.dynamic_slice_in_dim(own_pos, start, row_count, 1).T
    displace = near_pos[None, :, :] - mine[:, None, :]
    row_index = start + lax.broadcasted_iota(jnp.int32, (row_count, near_count), 0)
    col_index = lax.broadcasted_iota(jnp.int32, (row_count, near_count), 1)
    itself = (col_index == row_index + 13 * slots).astype(jnp.float32)
    distance = jnp.sqrt(jnp.sum(displace * displace, axis=-1) + itself)
    unit = displace / distance[:, :, None]
    smooth = jnp.where(distance < cutoff, 0.5 * (jnp.cos(math.pi * distance / cutoff) + 1.0), 0.0)
    weight = smooth * near_live[None, :] * (1.0 - itself)
    basis_count = radial_in.shape[0]
    centers = lax.broadcasted_iota(jnp.float32, (basis_count,), 0) * (cutoff / (basis_count - 1))
    sharpness = 0.5 * ((basis_count - 1) / cutoff) ** 2
    basis = jnp.exp(-sharpness * (distance[:, :, None] - centers) ** 2).astype(jnp.bfloat16)
    hidden = (
        jnp.dot(basis.reshape(-1, basis_count), radial_in, preferred_element_type=jnp.float32)
        + radial_bias
    )
    hidden = jax.nn.silu(hidden).reshape(row_count, near_count, -1) * weight[:, :, None]
    edge = jnp.concatenate(
        [hidden[:, :, None, :], hidden[:, :, None, :] * unit[:, :, :, None]], axis=2
    ).astype(jnp.bfloat16)
    edge_plain = edge[:, :, 0, :]
    edge_turned = edge[:, :, 1:, :]
    scalar_part = lax.dot_general(
        edge_plain, plain_side, (((1,), (0,)), ((), ())), preferred_element_type=jnp.float32
    )
    along_part = lax.dot_general(
        edge_turned, gate_c, (((1,), (0,)), ((), ())), preferred_element_type=jnp.float32
    )
    project_part = lax.dot_general(
        edge_turned, pair_g, (((1, 2), (0, 1)), ((), ())), preferred_element_type=jnp.float32
    )
    filters = radial_out.astype(jnp.float32).reshape(-1, 4, width)
    term_a = scalar_part[:, :, :width]
    term_b = scalar_part[:, :, width:].reshape(row_count, -1, 3, width)
    scalar_delta = message_scale * (
        jnp.sum(term_a * filters[None, :, 0, :], axis=1)
        + jnp.sum(project_part * filters[None, :, 3, :], axis=1)
    )
    vector_delta = message_scale * (
        jnp.sum(term_b * filters[None, :, None, 1, :], axis=1)
        + jnp.sum(along_part * filters[None, None, :, 2, :], axis=2)
    )
    return (scalar_delta, vector_delta)


def cell_deltas(cell, geo_pad, feat_pad, layer_params):
    radial_in, radial_bias, radial_out, atom_in, atom_bias, atom_out = layer_params
    cells_deep = geo_pad.shape[1] - 2
    cells_tall = geo_pad.shape[2] - 2
    slots = geo_pad.shape[4]
    width = feat_pad.shape[-1]
    at_x = cell // (cells_deep * cells_tall)
    at_y = cell // cells_tall % cells_deep
    at_z = cell % cells_tall
    zero = jnp.zeros((), jnp.int32)
    geo_near = lax.dynamic_slice(
        geo_pad, (at_x, at_y, at_z, zero, zero), (3, 3, 3) + geo_pad.shape[3:]
    ).reshape((27,) + geo_pad.shape[3:])
    feat_near = lax.dynamic_slice(
        feat_pad, (at_x, at_y, at_z, zero, zero, zero), (3, 3, 3) + feat_pad.shape[3:]
    ).reshape((27 * slots,) + feat_pad.shape[4:])
    near_pos = (
        (geo_near[:, :3, :] + offsets_table()[:, :, None] * cutoff)
        .transpose(0, 2, 1)
        .reshape(27 * slots, 3)
    )
    near_live = geo_near[:, 3, :].reshape(27 * slots)
    own_pos = geo_near[13, :3, :]
    gates = feat_near[:, :4, :]
    near_vectors = feat_near[:, 4:, :].astype(jnp.float32)
    pair_b = (gates[:, 1, None, :].astype(jnp.float32) * near_vectors).astype(jnp.bfloat16)
    pair_g = (gates[:, 3, None, :].astype(jnp.float32) * near_vectors).astype(jnp.bfloat16)
    plain_side = jnp.concatenate([gates[:, 0, :], pair_b.reshape(27 * slots, 3 * width)], axis=1)
    gate_c = gates[:, 2, :]
    row_count = slots // 8

    def compute_block(start):
        return receiver_block(
            start,
            row_count,
            near_pos,
            near_live,
            own_pos,
            plain_side,
            gate_c,
            pair_g,
            radial_in,
            radial_bias,
            radial_out,
        )

    def one_block(block):
        start = block * row_count
        return compute_block(start)

    scalar_delta, vector_delta = lax.map(one_block, jnp.arange(8, dtype=jnp.int32))
    return (scalar_delta.reshape(slots, width), vector_delta.reshape(slots, 3, width))


def all_deltas(geo_pad, feat_pad, layer_params, total_cells):

    def one_cell(cell):
        return cell_deltas(cell, geo_pad, feat_pad, layer_params)

    return lax.map(one_cell, jnp.arange(total_cells, dtype=jnp.int32))


def on_device(
    positions,
    counts,
    scalars,
    vectors,
    radial_in,
    radial_bias,
    radial_out,
    atom_in,
    atom_bias,
    atom_out,
    readout_in,
    readout_out,
):
    cells_wide, cells_deep, cells_tall, slots, width = scalars.shape
    total_cells = cells_wide * cells_deep * cells_tall
    live = (
        lax.broadcasted_iota(jnp.int32, (cells_wide, cells_deep, cells_tall, slots), 3)
        < counts[:, :, :, None]
    ).astype(jnp.float32)
    geometry = jnp.concatenate([positions, live[:, :, :, None, :]], axis=3)
    geo_pad = extended(geometry, (("gx", 0), ("gy", 1), ("gz", 2)), 1)
    scalar_state, vector_state = (scalars, vectors)
    for layer in range(radial_in.shape[0]):
        layer_params = (
            radial_in[layer],
            radial_bias[layer],
            radial_out[layer],
            atom_in[layer],
            atom_bias[layer],
            atom_out[layer],
        )
        own_gates = atom_gates(scalar_state, atom_in[layer], atom_bias[layer], atom_out[layer])
        stacked = jnp.concatenate([own_gates, vector_state], axis=4)
        feat_pad = extended(stacked, (("gx", 0), ("gy", 1), ("gz", 2)), 1)
        scalar_delta, vector_delta = all_deltas(geo_pad, feat_pad, layer_params, total_cells)
        scalar_delta = scalar_delta.reshape(cells_wide, cells_deep, cells_tall, slots, width)
        vector_delta = vector_delta.reshape(cells_wide, cells_deep, cells_tall, slots, 3, width)
        scalar_state = ((scalar_state.astype(jnp.float32) + scalar_delta) * live[..., None]).astype(
            jnp.bfloat16
        )
        vector_state = (
            (vector_state.astype(jnp.float32) + vector_delta) * live[..., None, None]
        ).astype(jnp.bfloat16)
    readout_hidden = jax.nn.silu(
        jnp.dot(scalar_state.reshape(-1, width), readout_in, preferred_element_type=jnp.float32)
    )
    atom_energy = jnp.sum(readout_hidden * readout_out, axis=-1) * live.reshape(-1)
    local_energy = jnp.sum(atom_energy)
    energy = lax.psum(local_energy, ("gx", "gy", "gz")).reshape(1)
    return (scalar_state, vector_state, energy)


def solution(mesh):
    in_specs = (
        P("gx", "gy", "gz", None, None),
        P("gx", "gy", "gz"),
        P("gx", "gy", "gz", None, None),
        P("gx", "gy", "gz", None, None, None),
        P(),
        P(),
        P(),
        P(),
        P(),
        P(),
        P(),
        P(),
    )
    out_specs = (P("gx", "gy", "gz", None, None), P("gx", "gy", "gz", None, None, None), P())
    return jax.shard_map(
        on_device, mesh=mesh, in_specs=in_specs, out_specs=out_specs, check_vma=False
    )
```

profile of v0, /device:TPU:1, one launch (start us, length us, event | category | flops | bytes accessed | tf_op | source)
XLA Modules:
  0.0 444.2 jit_solution(1733361480166152862)
XLA Ops:
  0.7 1.3 slice_bitcast_fusion.14
  1.9 1.2 convolution_convert_fusion.1
  4.0 5.0 %collective-permute-start.7 = (bf16[1,1,1,32,7,128]{5,3,2,1,0,4:T(8,128)(2,1)S(1)}, bf16[1,1,1,32,7,128]{5,3,2,1,0,4:T(8,128)(2,1)S(1)}, u32[]{:S(2)}, u32[]{:S(2)}) collective-permute-start(bf16[1,1,1,32,7,128]{5,3,2,1,0,4:T(8,128)(2,1)S(1)} %get-tuple-element.994), channel_id=1, source_target_pairs={{16,0},{32,16},{48,32},{64,48},{80,64},{96,80},{112,96},{0,112},{1... | collective-permute-start | bytes 172040 | tf_op jit(solution)/shard_map/ppermute | solution.py:21
  10.5 3.6 collective-permute-start.1
  14.2 2.2 collective-permute-start.9
  16.4 3.3 collective-permute-start.8
  19.7 1.3 slice_bitcast_fusion.12
  20.9 1.5 slice_bitcast_fusion.10
  22.4 2.7 collective-permute-done.9
  25.2 2.5 collective-permute-start.11
  27.8 1.7 collective-permute-start.3
  29.5 1.6 collective-permute-start.2
  32.4 2.7 collective-permute-start.5
  35.8 5.9 %collective-permute-done.5 = f32[4,3,1,4,32]{4,3,2,1,0:T(4,128)S(1)} collective-permute-done((f32[4,3,1,4,32]{4,3,2,1,0:T(4,128)S(1)}, f32[4,3,1,4,32]{4,3,2,1,0:T(4,128)S(1)}, u32[]{:S(2)}, u32[]{:S(2)}) %collective-permute-start.5) | collective-permute-done | bytes 6176 | tf_op jit(solution)/shard_map/ppermute | solution.py:21
  41.6 3.1 collective-permute-done.4
  45.4 1.5 pad_maximum_fusion.2
  48.7 142.8 %while.87 = (s32[]{:T(128)}, f32[2,32,128]{2,1,0:T(8,128)}, f32[2,32,3,128]{3,1,2,0:T(8,128)}, s32[2]{0:T(128)}, f32[4,3,3,4,32]{4,3,2,1,0:T(4,128)}, /*index=5*...) while((s32[]{:T(128)}, f32[2,32,128]{2,1,0:T(8,128)}, ...), condition=%wide.region_8.9_spmd, body=%wide.region_0.8_spmd.sunk | while | flops 578568832 | bytes 32141488 | solution.py:165
  48.7 1.2 dynamic_slice.94
  53.0 1.7 constant_dynamic-slice_fusion.15
  55.5 1.1 fusion.195
  57.8 60.2 %while.90 = (s32[]{:T(128)}, f32[8,4,128]{2,1,0:T(4,128)S(1)}, f32[8,4,3,128]{3,2,1,0:T(4,128)}, f32[27,32,3]{1,0,2:T(8,128)}, s32[8]{0:T(128)S(1)}, /*index=5*/...) while((s32[]{:T(128)}, f32[8,4,128]{2,1,0:T(4,128)S(1)}, ...), condition=%wide.wide.region_7.7_spmd, body=%wide.wide.region_1.6_spmd.sunk | while | flops 574914944 | bytes 18360236 | solution.py:156
  118.6 1.5 copy_dynamic-update-slice_fusion.8
  120.1 1.2 dynamic_slice.94
  124.4 1.7 constant_dynamic-slice_fusion.15
  129.2 60.2 %while.90 = (s32[]{:T(128)}, f32[8,4,128]{2,1,0:T(4,128)S(1)}, f32[8,4,3,128]{3,2,1,0:T(4,128)}, f32[27,32,3]{1,0,2:T(8,128)}, s32[8]{0:T(128)S(1)}, /*index=5*/...) while((s32[]{:T(128)}, f32[8,4,128]{2,1,0:T(4,128)S(1)}, ...), condition=%wide.wide.region_7.7_spmd, body=%wide.wide.region_1.6_spmd.sunk | while | flops 574914944 | bytes 18360236 | solution.py:156
  190.0 1.5 copy_dynamic-update-slice_fusion.8
  192.9 1.2 convolution_convert_fusion
  195.2 1.9 collective-permute-start.13
  197.2 1.3 collective-permute-done.13
  198.4 3.9 collective-permute-done.12
  202.3 4.6 %collective-permute-start.15 = (bf16[4,1,1,32,7,128]{5,3,2,1,0,4:T(8,128)(2,1)S(1)}, bf16[4,1,1,32,7,128]{5,3,2,1,0,4:T(8,128)(2,1)S(1)}, u32[]{:S(2)}, u32[]{:S(2)}) collective-permute-start(bf16[4,1,1,32,7,128]{5,3,2,1,0,4:T(8,128)(2,1)S(1)} %pad_maximum_fusion.7), channel_id=1, source_target_pairs={{4,0},{8,4},{12,8},{0,12},{5,1},{9,5},{13,9},{1,13},{6,2},{10,6},{... | collective-permute-start | bytes 688136 | tf_op jit(solution)/shard_map/ppermute | solution.py:21
  206.9 2.2 collective-permute-start.14
  209.1 6.0 %collective-permute-done.15 = bf16[4,1,1,32,7,128]{5,3,2,1,0,4:T(8,128)(2,1)S(1)} collective-permute-done((bf16[4,1,1,32,7,128]{5,3,2,1,0,4:T(8,128)(2,1)S(1)}, bf16[4,1,1,32,7,128]{5,3,2,1,0,4:T(8,128)(2,1)S(1)}, u32[]{:S(2)}, u32[]{:S(2)}) %collective-permute-start.15) | collective-permute-done | bytes 229408 | tf_op jit(solution)/shard_map/ppermute | solution.py:21
  215.2 1.5 collective-permute-start.16
  218.1 13.3 %collective-permute-done.17 = bf16[4,3,1,32,7,128]{5,3,2,1,0,4:T(8,128)(2,1)S(1)} collective-permute-done((bf16[4,3,1,32,7,128]{5,3,2,1,0,4:T(8,128)(2,1)S(1)}, bf16[4,3,1,32,7,128]{5,3,2,1,0,4:T(8,128)(2,1)S(1)}, u32[]{:S(2)}, u32[]{:S(2)}) %collective-permute-start.17) | collective-permute-done | bytes 688160 | tf_op jit(solution)/shard_map/ppermute | solution.py:21
  232.4 1.5 pad_maximum_fusion.3
  235.7 140.5 %while.89 = (s32[]{:T(128)}, f32[2,32,128]{2,1,0:T(8,128)}, f32[2,32,3,128]{3,1,2,0:T(8,128)}, s32[2]{0:T(128)}, f32[4,3,3,4,32]{4,3,2,1,0:T(4,128)}, /*index=5*...) while((s32[]{:T(128)}, f32[2,32,128]{2,1,0:T(8,128)}, ...), condition=%wide.region_17.18_spmd, body=%wide.region_9.17_spmd.sunk | while | flops 578568832 | bytes 32139408 | solution.py:165
  235.7 1.2 dynamic_slice.97
  240.0 1.7 constant_dynamic-slice_fusion.17
  244.8 59.1 %while.91 = (s32[]{:T(128)}, f32[8,4,128]{2,1,0:T(4,128)S(1)}, f32[8,4,3,128]{3,2,1,0:T(4,128)}, f32[27,32,3]{1,0,2:T(8,128)}, s32[8]{0:T(128)S(1)}, /*index=5*/...) while((s32[]{:T(128)}, f32[8,4,128]{2,1,0:T(4,128)S(1)}, ...), condition=%wide.wide.region_16.16_spmd, body=%wide.wide.region_10.15_spmd.sunk | while | flops 574914944 | bytes 18358132 | solution.py:156
  304.5 1.5 copy_dynamic-update-slice_fusion.9
  306.0 1.2 dynamic_slice.97
  310.3 1.7 constant_dynamic-slice_fusion.17
  315.0 59.1 %while.91 = (s32[]{:T(128)}, f32[8,4,128]{2,1,0:T(4,128)S(1)}, f32[8,4,3,128]{3,2,1,0:T(4,128)}, f32[27,32,3]{1,0,2:T(8,128)}, s32[8]{0:T(128)S(1)}, /*index=5*/...) while((s32[]{:T(128)}, f32[8,4,128]{2,1,0:T(4,128)S(1)}, ...), condition=%wide.wide.region_16.16_spmd, body=%wide.wide.region_10.15_spmd.sunk | while | flops 574914944 | bytes 18358132 | solution.py:156
  374.7 1.5 copy_dynamic-update-slice_fusion.9
  377.0 1.6 fusion.91
  379.5 1.3 fusion.117
  380.8 63.4 %psum.7 = f32[1]{0:T(128)} all-reduce(f32[1]{0:T(128)} %bitcast.76), channel_id=1, replica_groups=mesh['gx'=8,'gy'=4,'gz'=4] {'gx','gy','gz'}, use_global_device_ids=true, to_apply=%region_20.21 | all-reduce | flops 1 | bytes 8 | tf_op jit(solution)/shard_map/psum | solution.py:217
  (1392 shorter events, 245.7 us)
Async XLA Ops:
  0.6 378.0 %copy-start = (bf16[128,64]{0,1:T(8,128)(2,1)S(1)}, bf16[128,64]{0,1:T(8,128)(2,1)}, u32[]{:S(2)}) copy-start(bf16[128,64]{0,1:T(8,128)(2,1)} %param.30) | copy-start | bytes 49156
  0.6 34.5 %copy-start.19 = (s32[2,1,1]{0,2,1:T(1,128)S(1)}, s32[2,1,1]{0,2,1:T(1,128)}, u32[]{:S(2)}) copy-start(s32[2,1,1]{0,2,1:T(1,128)} %param.21) | copy-start | bytes 28
  0.7 30.4 %copy-start.14 = (f32[2,64]{1,0:T(2,128)S(1)}, f32[2,64]{1,0:T(2,128)}, u32[]{:S(2)}) copy-start(f32[2,64]{1,0:T(2,128)} %param.25) | copy-start | bytes 1540
  4.0 10.1 %collective-permute-start.7 = (bf16[1,1,1,32,7,128]{5,3,2,1,0,4:T(8,128)(2,1)S(1)}, bf16[1,1,1,32,7,128]{5,3,2,1,0,4:T(8,128)(2,1)S(1)}, u32[]{:S(2)}, u32[]{:S(2)}) collective-permute-start(bf16[1,1,1,32,7,128]{5,3,2,1,0,4:T(8,128)(2,1)S(1)} %get-tuple-element.994), channel_id=1, source_target_pairs={{16,0},{32,16},{48,32},{64,48},{80,64},{96,80},{112,96},{0,112},{1... | collective-permute-start | bytes 172040 | tf_op jit(solution)/shard_map/ppermute | solution.py:21
  9.0 5.1 %collective-permute-start.6 = (bf16[1,1,1,32,7,128]{5,3,2,1,0,4:T(8,128)(2,1)S(1)}, bf16[1,1,1,32,7,128]{5,3,2,1,0,4:T(8,128)(2,1)S(1)}, u32[]{:S(2)}, u32[]{:S(2)}) collective-permute-start(bf16[1,1,1,32,7,128]{5,3,2,1,0,4:T(8,128)(2,1)S(1)} %get-tuple-element.993), channel_id=1, source_target_pairs={{0,16},{16,32},{32,48},{48,64},{64,80},{80,96},{96,112},{112,0},{1... | collective-permute-start | bytes 172040 | tf_op jit(solution)/shard_map/ppermute | solution.py:18
  10.5 17.3 %collective-permute-start.1 = (f32[1,1,1,4,32]{4,3,2,1,0:T(4,128)S(1)}, f32[1,1,1,4,32]{4,3,2,1,0:T(4,128)S(1)}, u32[]{:S(2)}, u32[]{:S(2)}) collective-permute-start(f32[1,1,1,4,32]{4,3,2,1,0:T(4,128)S(1)} %get-tuple-element.996), channel_id=1, source_target_pairs={{16,0},{32,16},{48,32},{64,48},{80,64},{96,80},{112,96},{0,112},{1... | collective-permute-start | bytes 1544 | tf_op jit(solution)/shard_map/ppermute | solution.py:21
  14.1 13.6 %collective-permute-start = (f32[1,1,1,4,32]{4,3,2,1,0:T(4,128)S(1)}, f32[1,1,1,4,32]{4,3,2,1,0:T(4,128)S(1)}, u32[]{:S(2)}, u32[]{:S(2)}) collective-permute-start(f32[1,1,1,4,32]{4,3,2,1,0:T(4,128)S(1)} %get-tuple-element.995), channel_id=1, source_target_pairs={{0,16},{16,32},{32,48},{48,64},{64,80},{80,96},{96,112},{112,0},{1... | collective-permute-start | bytes 1544 | tf_op jit(solution)/shard_map/ppermute | solution.py:18
  14.2 10.9 %collective-permute-start.9 = (bf16[4,1,1,32,7,128]{5,3,2,1,0,4:T(8,128)(2,1)S(1)}, bf16[4,1,1,32,7,128]{5,3,2,1,0,4:T(8,128)(2,1)S(1)}, u32[]{:S(2)}, u32[]{:S(2)}) collective-permute-start(bf16[4,1,1,32,7,128]{5,3,2,1,0,4:T(8,128)(2,1)S(1)} %pad_maximum_fusion.6), channel_id=1, source_target_pairs={{4,0},{8,4},{12,8},{0,12},{5,1},{9,5},{13,9},{1,13},{6,2},{10,6},{... | collective-permute-start | bytes 688136 | tf_op jit(solution)/shard_map/ppermute | solution.py:21
  16.4 8.7 %collective-permute-start.8 = (bf16[4,1,1,32,7,128]{5,3,2,1,0,4:T(8,128)(2,1)S(1)}, bf16[4,1,1,32,7,128]{5,3,2,1,0,4:T(8,128)(2,1)S(1)}, u32[]{:S(2)}, u32[]{:S(2)}) collective-permute-start(bf16[4,1,1,32,7,128]{5,3,2,1,0,4:T(8,128)(2,1)S(1)} %pad_maximum_fusion.6), channel_id=1, source_target_pairs={{0,4},{4,8},{8,12},{12,0},{1,5},{5,9},{9,13},{13,1},{2,6},{6,10},{... | collective-permute-start | bytes 688136 | tf_op jit(solution)/shard_map/ppermute | solution.py:18
  25.2 20.2 %collective-permute-start.11 = (bf16[4,3,1,32,7,128]{5,3,2,1,0,4:T(8,128)(2,1)S(1)}, bf16[4,3,1,32,7,128]{5,3,2,1,0,4:T(8,128)(2,1)S(1)}, u32[]{:S(2)}, u32[]{:S(2)}) collective-permute-start(bf16[4,3,1,32,7,128]{5,3,2,1,0,4:T(8,128)(2,1)S(1)} %pad_maximum_fusion.4), channel_id=1, source_target_pairs={{1,0},{2,1},{3,2},{0,3},{5,4},{6,5},{7,6},{4,7},{9,8},{10,9},{11,1... | collective-permute-start | bytes 2064392 | tf_op jit(solution)/shard_map/ppermute | solution.py:21
  27.7 17.7 %collective-permute-start.10 = (bf16[4,3,1,32,7,128]{5,3,2,1,0,4:T(8,128)(2,1)S(1)}, bf16[4,3,1,32,7,128]{5,3,2,1,0,4:T(8,128)(2,1)S(1)}, u32[]{:S(2)}, u32[]{:S(2)}) collective-permute-start(bf16[4,3,1,32,7,128]{5,3,2,1,0,4:T(8,128)(2,1)S(1)} %pad_maximum_fusion.4), channel_id=1, source_target_pairs={{0,1},{1,2},{2,3},{3,0},{4,5},{5,6},{6,7},{7,4},{8,9},{9,10},{10,1... | collective-permute-start | bytes 2064392 | tf_op jit(solution)/shard_map/ppermute | solution.py:18
  27.8 4.6 %collective-permute-start.3 = (f32[4,1,1,4,32]{4,3,2,1,0:T(4,128)S(1)}, f32[4,1,1,4,32]{4,3,2,1,0:T(4,128)S(1)}, u32[]{:S(2)}, u32[]{:S(2)}) collective-permute-start(f32[4,1,1,4,32]{4,3,2,1,0:T(4,128)S(1)} %pad_maximum_fusion.10), channel_id=1, source_target_pairs={{4,0},{8,4},{12,8},{0,12},{5,1},{9,5},{13,9},{1,13},{6,2},{10,6},{... | collective-permute-start | bytes 6152 | tf_op jit(solution)/shard_map/ppermute | solution.py:21
  29.5 3.0 collective-permute-start.2
  32.4 9.2 %collective-permute-start.5 = (f32[4,3,1,4,32]{4,3,2,1,0:T(4,128)S(1)}, f32[4,3,1,4,32]{4,3,2,1,0:T(4,128)S(1)}, u32[]{:S(2)}, u32[]{:S(2)}) collective-permute-start(f32[4,3,1,4,32]{4,3,2,1,0:T(4,128)S(1)} %pad_maximum_fusion.9), channel_id=1, source_target_pairs={{1,0},{2,1},{3,2},{0,3},{5,4},{6,5},{7,6},{4,7},{9,8},{10,9},{11,1... | collective-permute-start | bytes 18440 | tf_op jit(solution)/shard_map/ppermute | solution.py:21
  35.2 9.6 %collective-permute-start.4 = (f32[4,3,1,4,32]{4,3,2,1,0:T(4,128)S(1)}, f32[4,3,1,4,32]{4,3,2,1,0:T(4,128)S(1)}, u32[]{:S(2)}, u32[]{:S(2)}) collective-permute-start(f32[4,3,1,4,32]{4,3,2,1,0:T(4,128)S(1)} %pad_maximum_fusion.9), channel_id=1, source_target_pairs={{0,1},{1,2},{2,3},{3,0},{4,5},{5,6},{6,7},{7,4},{8,9},{9,10},{10,1... | collective-permute-start | bytes 18440 | tf_op jit(solution)/shard_map/ppermute | solution.py:18
  48.7 142.8 %copy-start.10 = (f32[2,32]{1,0:T(2,128)S(1)}, f32[2,32]{1,0:T(2,128)}, u32[]{:S(2)}) copy-start(f32[2,32]{1,0:T(2,128)} %compare_convert_fusion.1) | copy-start | bytes 772
  48.7 144.3 %copy-start.16 = (f32[128]{0:T(128)S(1)}, f32[128]{0:T(128)}, u32[]{:S(2)}) copy-start(f32[128]{0:T(128)} %get-tuple-element.1001) | copy-start | bytes 1540
  53.0 4.8 %copy-start.6 = (f32[27,32,3]{1,0,2:T(8,128)}, f32[27,32,3]{1,0,2:T(8,128)S(1)}, u32[]{:S(2)}) copy-start(f32[27,32,3]{1,0,2:T(8,128)S(1)} %copy.256) | copy-start | bytes 31108 | tf_op jit(solution)/shard_map/while
  57.8 2.1 copy-start.17
  57.8 2.1 copy-start.21
  65.4 2.1 copy-start.21
  72.9 2.1 copy-start.21
  80.4 2.1 copy-start.21
  87.9 2.1 copy-start.21
  95.4 2.1 copy-start.21
  103.0 2.1 copy-start.21
  110.5 2.1 copy-start.21
  124.4 4.8 %copy-start.6 = (f32[27,32,3]{1,0,2:T(8,128)}, f32[27,32,3]{1,0,2:T(8,128)S(1)}, u32[]{:S(2)}) copy-start(f32[27,32,3]{1,0,2:T(8,128)S(1)} %copy.256) | copy-start | bytes 31108 | tf_op jit(solution)/shard_map/while
  129.2 2.1 copy-start.17
  129.2 2.1 copy-start.21
  136.8 2.1 copy-start.21
  144.3 2.1 copy-start.21
  174.4 2.1 copy-start.21
  191.5 25.8 %copy-start.20 = (s32[2,1,1]{0,2,1:T(1,128)S(1)}, s32[2,1,1]{0,2,1:T(1,128)}, u32[]{:S(2)}) copy-start(s32[2,1,1]{0,2,1:T(1,128)} %param.21) | copy-start | bytes 28
  195.2 19.9 %copy-start.8 = (bf16[2,1,1,32,3,128]{5,3,4,2,1,0:T(8,128)(2,1)}, bf16[2,1,1,32,3,128]{5,3,4,2,1,0:T(8,128)(2,1)S(1)}, u32[]{:S(2)}) copy-start(bf16[2,1,1,32,3,128]{5,3,4,2,1,0:T(8,128)(2,1)S(1)} %fusion.93) | copy-start | bytes 147460
  195.2 3.2 collective-permute-start.13
  197.2 5.1 %collective-permute-start.12 = (bf16[1,1,1,32,7,128]{5,3,2,1,0,4:T(8,128)(2,1)S(1)}, bf16[1,1,1,32,7,128]{5,3,2,1,0,4:T(8,128)(2,1)S(1)}, u32[]{:S(2)}, u32[]{:S(2)}) collective-permute-start(bf16[1,1,1,32,7,128]{5,3,2,1,0,4:T(8,128)(2,1)S(1)} %get-tuple-element.991), channel_id=1, source_target_pairs={{0,16},{16,32},{32,48},{48,64},{64,80},{80,96},{96,112},{112,0},{1... | collective-permute-start | bytes 172040 | tf_op jit(solution)/shard_map/ppermute | solution.py:18
  202.3 12.7 %collective-permute-start.15 = (bf16[4,1,1,32,7,128]{5,3,2,1,0,4:T(8,128)(2,1)S(1)}, bf16[4,1,1,32,7,128]{5,3,2,1,0,4:T(8,128)(2,1)S(1)}, u32[]{:S(2)}, u32[]{:S(2)}) collective-permute-start(bf16[4,1,1,32,7,128]{5,3,2,1,0,4:T(8,128)(2,1)S(1)} %pad_maximum_fusion.7), channel_id=1, source_target_pairs={{4,0},{8,4},{12,8},{0,12},{5,1},{9,5},{13,9},{1,13},{6,2},{10,6},{... | collective-permute-start | bytes 688136 | tf_op jit(solution)/shard_map/ppermute | solution.py:21
  206.9 8.2 %collective-permute-start.14 = (bf16[4,1,1,32,7,128]{5,3,2,1,0,4:T(8,128)(2,1)S(1)}, bf16[4,1,1,32,7,128]{5,3,2,1,0,4:T(8,128)(2,1)S(1)}, u32[]{:S(2)}, u32[]{:S(2)}) collective-permute-start(bf16[4,1,1,32,7,128]{5,3,2,1,0,4:T(8,128)(2,1)S(1)} %pad_maximum_fusion.7), channel_id=1, source_target_pairs={{0,4},{4,8},{8,12},{12,0},{1,5},{5,9},{9,13},{13,1},{2,6},{6,10},{... | collective-permute-start | bytes 688136 | tf_op jit(solution)/shard_map/ppermute | solution.py:18
  215.2 16.2 %collective-permute-start.17 = (bf16[4,3,1,32,7,128]{5,3,2,1,0,4:T(8,128)(2,1)S(1)}, bf16[4,3,1,32,7,128]{5,3,2,1,0,4:T(8,128)(2,1)S(1)}, u32[]{:S(2)}, u32[]{:S(2)}) collective-permute-start(bf16[4,3,1,32,7,128]{5,3,2,1,0,4:T(8,128)(2,1)S(1)} %pad_maximum_fusion.5), channel_id=1, source_target_pairs={{1,0},{2,1},{3,2},{0,3},{5,4},{6,5},{7,6},{4,7},{9,8},{10,9},{11,1... | collective-permute-start | bytes 2064392 | tf_op jit(solution)/shard_map/ppermute | solution.py:21
  215.2 17.2 %collective-permute-start.16 = (bf16[4,3,1,32,7,128]{5,3,2,1,0,4:T(8,128)(2,1)S(1)}, bf16[4,3,1,32,7,128]{5,3,2,1,0,4:T(8,128)(2,1)S(1)}, u32[]{:S(2)}, u32[]{:S(2)}) collective-permute-start(bf16[4,3,1,32,7,128]{5,3,2,1,0,4:T(8,128)(2,1)S(1)} %pad_maximum_fusion.5), channel_id=1, source_target_pairs={{0,1},{1,2},{2,3},{3,0},{4,5},{5,6},{6,7},{7,4},{8,9},{9,10},{10,1... | collective-permute-start | bytes 2064392 | tf_op jit(solution)/shard_map/ppermute | solution.py:18
  218.1 17.6 %copy-start.1 = (bf16[64,512]{1,0:T(8,128)(2,1)S(1)}, bf16[64,512]{1,0:T(8,128)(2,1)}, u32[]{:S(2)}) copy-start(bf16[64,512]{1,0:T(8,128)(2,1)} %get-tuple-element.1726) | copy-start | bytes 196612
  218.1 17.6 %copy-start.13 = (bf16[8,64]{1,0:T(8,128)(2,1)S(1)}, bf16[8,64]{1,0:T(8,128)(2,1)}, u32[]{:S(2)}) copy-start(bf16[8,64]{1,0:T(8,128)(2,1)} %get-tuple-element.1724) | copy-start | bytes 3076
  218.1 17.6 %copy-start.15 = (f32[1,64]{1,0:T(1,128)S(1)}, f32[1,64]{1,0:T(1,128)}, u32[]{:S(2)}) copy-start(f32[1,64]{1,0:T(1,128)} %get-tuple-element.1725) | copy-start | bytes 772
  235.7 140.5 %copy-start.11 = (f32[2,32]{1,0:T(2,128)S(1)}, f32[2,32]{1,0:T(2,128)}, u32[]{:S(2)}) copy-start(f32[2,32]{1,0:T(2,128)} %compare_convert_fusion.1) | copy-start | bytes 772
  239.9 4.7 %copy-start.7 = (f32[27,32,3]{1,0,2:T(8,128)}, f32[27,32,3]{1,0,2:T(8,128)S(1)}, u32[]{:S(2)}) copy-start(f32[27,32,3]{1,0,2:T(8,128)S(1)} %copy.261) | copy-start | bytes 31108 | tf_op jit(solution)/shard_map/while
  310.2 4.7 %copy-start.7 = (f32[27,32,3]{1,0,2:T(8,128)}, f32[27,32,3]{1,0,2:T(8,128)S(1)}, u32[]{:S(2)}) copy-start(f32[27,32,3]{1,0,2:T(8,128)S(1)} %copy.261) | copy-start | bytes 31108 | tf_op jit(solution)/shard_map/while
  377.0 67.1 %copy-start.12 = (bf16[2,1,1,32,128]{4,3,2,1,0:T(8,128)(2,1)}, bf16[2,1,1,32,128]{4,3,2,1,0:T(8,128)(2,1)S(1)}, u32[]{:S(2)}) copy-start(bf16[2,1,1,32,128]{4,3,2,1,0:T(8,128)(2,1)S(1)} %fusion.95) | copy-start | bytes 49156
  (147 other events, 243.6 us)
where the time goes:
time: 447 us; the launch traced here: 444 us
  local copies, waits for them, and re-layouts  149 us (33%)
  matrix products  67.1 us (15%)
  blocking collectives  63.4 us (14%)
  other arithmetic  58.9 us (13%)
  waiting for transfers between devices  37.9 us (8%)
  loops' own time  34.5 us (8%)
  starting transfers between devices  32.9 us (7%)
    psum x1, blocking collectives, on_device(): energy = lax.psum(local_energy, ('gx', 'gy', 'gz')).reshape(1)  63.4 us
    reshape x64, local copies, waits for them, and re-layouts, receiver_block(): jax.nn.silu(hidden).reshape(row_count, near_count, -1) * weight[:, :, None]  40.2 us
    while x392, local copies, waits for them, and re-layouts  30.4 us
    ppermute x9, waiting for transfers between devices, extended(): lax.ppermute(lax.slice_in_dim(block, 0, width, axis=dim), axis, backward)  29.8 us
    another operation x4, loops' own time, cell_deltas(): lax.map(one_block, jnp.arange(8, dtype=jnp.int32))  26.3 us
    ppermute x9, starting transfers between devices, extended(): lax.ppermute(lax.slice_in_dim(block, 0, width, axis=dim), axis, backward)  24.4 us
    dynamic_slice x32, local copies, waits for them, and re-layouts, cell_deltas(): lax.map(one_block, jnp.arange(8, dtype=jnp.int32))  21 us
    dynamic_update_slice x64, other arithmetic, cell_deltas(): lax.map(one_block, jnp.arange(8, dtype=jnp.int32))  19.8 us
  transfers between devices with their start and end apart: 18, of which 10 were waited for; matrix products, arithmetic and copies ran while one was open for 2% of the time, Pallas kernels for 0%

commit v1 on v0

v1 whole, which is shorter than its diff:
```python
import functools
import math

import jax
import jax.numpy as jnp
from jax import lax
from jax.experimental import pallas as pl
from jax.experimental.pallas import tpu as pltpu
from jax.sharding import PartitionSpec as P

cutoff = 5.0
message_scale = 0.5
slots = 32
chan = 128
hidden = 64
planes = 4
columns = 9
near = planes * columns * slots
span = 896
starts = (0, 256)
block = 8
f32 = jnp.float32
bf16 = jnp.bfloat16


def pieces(value):
    high = lax.reduce_precision(value, 8, 7)
    rest = value - high
    middle = lax.reduce_precision(rest, 8, 7)
    low = lax.reduce_precision(rest - middle, 8, 7)
    return high.astype(bf16), middle.astype(bf16), low.astype(bf16)


def dot(a, b):
    return jnp.dot(a, b, preferred_element_type=f32)


def half_silu(y):
    return y + y * jnp.tanh(y)


def layer_kernel(
    last,
    counts_ref,
    offs_ref,
    *refs,
):
    cols = refs[:columns]
    geo_in = None
    refs = refs[columns:]
    if last:
        geo_in = refs[0]
        refs = refs[1:]
    (rin_ref, rout_ref, ain_ref, abias_ref, aout_ref), refs = refs[:5], refs[5:]
    if last:
        (read_in_ref, read_out_ref), refs = refs[:2], refs[2:]
        state_ref, energy_ref = refs[:2]
        refs = refs[2:]
    else:
        state_ref, geo_out = refs[:2]
        refs = refs[2:]
    f0, f1, f2, f3, gall, pos, own, basis_s, wts_s, e0, e1, e2, e3, delta = refs
    fk = (f1, f2, f3)
    ek = (e1, e2, e3)

    for c in range(columns):
        x = cols[c][...].reshape(planes * slots, -1)
        s = x[:, :chan]
        hid = half_silu(0.5 * (dot(s, ain_ref[...]) + abias_ref[...])).astype(bf16)
        gates = dot(hid, aout_ref[...]).astype(bf16)
        ga, gb = gates[:, :chan], gates[:, chan : 2 * chan]
        gc, gg = gates[:, 2 * chan : 3 * chan], gates[:, 3 * chan :]
        vec = [x[:, (k + 1) * chan : (k + 2) * chan] for k in range(3)]
        row0 = jnp.concatenate([ga] + [gb * v for v in vec], axis=1)
        rows = [jnp.concatenate([gc, gg * v], axis=1) for v in vec]
        for p in range(planes):
            at = pl.ds((p * columns + c) * slots, slots)
            part = slice(p * slots, (p + 1) * slots)
            f0[at, :] = row0[part]
            for k in range(3):
                fk[k][at, :] = rows[k][part]
            if not last:
                gall[at, :] = x[part, 4 * chan :]
    if last:
        pos[...] = geo_in[0:8, :]
        own[...] = geo_in[8:72, :chan]
    else:
        lane = lax.broadcasted_iota(jnp.int32, (8, chan), 1)
        row = lax.broadcasted_iota(jnp.int32, (8, chan), 0)
        pick = (lane == row) | (lane == row + 8) | (lane == row + 16)
        pick = jnp.where(pick, 1.0, 0.0).astype(bf16)
        contract = (((1,), (1,)), ((), ()))
        pos[...] = lax.dot_general(pick, gall[...], contract, preferred_element_type=f32)
        lane = lax.broadcasted_iota(jnp.int32, (chan, chan), 1)
        row = lax.broadcasted_iota(jnp.int32, (chan, chan), 0)
        pick = (lane == row) | (lane + 8 == row) | (lane + 16 == row)
        pick = jnp.where(pick, 1.0, 0.0).astype(bf16)
        mine = cols[4][1:3].reshape(2 * slots, -1)[:, 4 * chan :]
        own[...] = dot(mine, pick)
        geo_out[0:8, :] = pos[...]
        geo_out[8:72, :chan] = own[...]
        geo_out[8:72, chan:] = jnp.zeros((2 * slots, near - chan), f32)
    delta[...] = jnp.zeros_like(delta)

    for q in range(2):
        window = slice(starts[q], starts[q] + span)
        dist2 = None
        disp = []
        for k in range(3):
            other = pos[k : k + 1, window] + offs_ref[q * 3 + k : q * 3 + k + 1, window]
            d = other - own[q * slots : (q + 1) * slots, k : k + 1]
            disp.append(d)
            dist2 = d * d if k == 0 else dist2 + d * d
        lane = lax.broadcasted_iota(jnp.int32, (slots, span), 1) + starts[q]
        row = lax.broadcasted_iota(jnp.int32, (slots, span), 0)
        self_at = ((1 + q) * columns + 4) * slots
        itself = jnp.where(lane == row + self_at, 1.0, 0.0)
        dist = jnp.sqrt(dist2 + itself)
        smooth = jnp.where(
            dist < cutoff, 0.5 * (jnp.cos(math.pi * dist / cutoff) + 1.0), 0.0
        )
        weight = smooth * pos[3:4, window] * (1.0 - itself)
        scaled = weight / dist
        wts_s[:, 0, :] = weight
        for k in range(3):
            wts_s[:, 1 + k, :] = scaled * disp[k]
        sharp = 0.5 * (7.0 / cutoff) ** 2
        for k in range(8):
            away = dist - k * (cutoff / 7.0)
            basis_s[:, k, :] = jnp.exp(-sharp * (away * away))

        def one_block(b, carry, q=q, window=window):
            for r in range(block):
                i = b * block + r
                wide = jnp.concatenate(
                    [basis_s[i], jnp.ones((8, span), f32)], axis=0
                ).astype(bf16)
                s = half_silu(dot(rin_ref[...], wide))
                part = slice(r * hidden, (r + 1) * hidden)
                w = wts_s[i]
                e0[part, :] = (s * w[0:1, :]).astype(bf16)
                for k in range(3):
                    ek[k][part, :] = (s * w[1 + k : 2 + k, :]).astype(bf16)
            plain = dot(e0[...], f0[window, :])
            turned = [dot(ek[k][...], fk[k][window, :]) for k in range(3)]
            radial = [rout_ref[:, g * chan : (g + 1) * chan][None] for g in range(4)]
            split = (block, hidden, chan)
            proj = turned[0][:, chan:] + turned[1][:, chan:] + turned[2][:, chan:]
            totals = [
                plain[:, :chan].reshape(split) * radial[0] + proj.reshape(split) * radial[3]
            ]
            for k in range(3):
                totals.append(
                    plain[:, (k + 1) * chan : (k + 2) * chan].reshape(split) * radial[1]
                    + turned[k][:, :chan].reshape(split) * radial[2]
                )
            at = pl.ds(pl.multiple_of(q * slots + b * block, block), block)
            for g in range(4):
                delta[at, g * chan : (g + 1) * chan] = jnp.sum(totals[g], axis=1)
            return carry

        blocks = (counts_ref[q] + block - 1) // block
        lax.fori_loop(0, blocks, one_block, 0)

    slot = lax.broadcasted_iota(jnp.int32, (2 * slots, 1), 0)
    limit = jnp.where(slot < slots, counts_ref[0], counts_ref[1] + slots)
    live = jnp.where(slot < limit, 1.0, 0.0)
    mine = cols[4][1:3].reshape(2 * slots, -1)[:, : 4 * chan].astype(f32)
    state = ((mine + message_scale * delta[...]) * live).astype(bf16)
    state_ref[...] = state
    if last:
        x = dot(state[:, :chan], read_in_ref[...])
        each = half_silu(0.5 * x) * read_out_ref[...] * live
        energy_ref[...] = jnp.broadcast_to(jnp.sum(each, keepdims=True), energy_ref.shape)


def layer_call(last, counts, offs, cols, geo, weights):
    vmem = pl.BlockSpec(memory_space=pltpu.VMEM)
    smem = pl.BlockSpec(memory_space=pltpu.SMEM)
    operands = [counts, offs] + list(cols) + ([geo] if last else []) + list(weights)
    state = jax.ShapeDtypeStruct((2 * slots, 4 * chan), bf16)
    if last:
        out = (state, jax.ShapeDtypeStruct((chan, chan), f32))
    else:
        out = (state, jax.ShapeDtypeStruct((72, near), f32))
    return pl.pallas_call(
        functools.partial(layer_kernel, last),
        out_shape=out,
        in_specs=[smem] + [vmem] * (len(operands) - 1),
        out_specs=(vmem, vmem),
        scratch_shapes=[
            pltpu.VMEM((near, 4 * chan), bf16),
            pltpu.VMEM((near, 2 * chan), bf16),
            pltpu.VMEM((near, 2 * chan), bf16),
            pltpu.VMEM((near, 2 * chan), bf16),
            pltpu.VMEM((near, chan), bf16),
            pltpu.VMEM((8, near), f32),
            pltpu.VMEM((2 * slots, chan), f32),
            pltpu.VMEM((slots, 8, span), f32),
            pltpu.VMEM((slots, 8, span), f32),
            pltpu.VMEM((block * hidden, span), bf16),
            pltpu.VMEM((block * hidden, span), bf16),
            pltpu.VMEM((block * hidden, span), bf16),
            pltpu.VMEM((block * hidden, span), bf16),
            pltpu.VMEM((2 * slots, 4 * chan), f32),
        ],
        compiler_params=pltpu.CompilerParams(vmem_limit_bytes=48 * 1024 * 1024),
        name="layer_last" if last else "layer_first",
    )(*operands)


def exchange(own):
    count = lax.axis_size("gx")
    up = [(i, (i + 1) % count) for i in range(count)]
    down = [(i, (i - 1) % count) for i in range(count)]
    low = lax.ppermute(own[1:2], "gx", up)
    high = lax.ppermute(own[0:1], "gx", down)
    column = jnp.concatenate([low, own, high], axis=0)
    deep, tall = lax.axis_size("gy"), lax.axis_size("gz")
    cols = []
    for dy in (-1, 0, 1):
        for dz in (-1, 0, 1):
            if dy == 0 and dz == 0:
                cols.append(column)
                continue
            pairs = [
                (((y + dy) % deep) * tall + (z + dz) % tall, y * tall + z)
                for y in range(deep)
                for z in range(tall)
            ]
            cols.append(lax.ppermute(column, ("gy", "gz"), pairs))
    return cols


def offsets():
    rows = []
    lane = lax.broadcasted_iota(jnp.int32, (near,), 0) // slots
    plane, col = lane // columns, lane % columns
    for q in range(2):
        rows += [plane - 1 - q, col // 3 - 1, col % 3 - 1]
    rows += [plane * 0, plane * 0]
    return jnp.stack(rows).astype(f32) * cutoff


def on_device(
    positions,
    counts,
    scalars,
    vectors,
    radial_in,
    radial_bias,
    radial_out,
    atom_in,
    atom_bias,
    atom_out,
    readout_in,
    readout_out,
):
    counts = counts.reshape(2)
    live = (lax.broadcasted_iota(jnp.int32, (2, slots), 1) < counts[:, None]).astype(f32)
    geo = jnp.concatenate([positions.reshape(2, 3, slots), live[:, None, :]], axis=1)
    geo = jnp.pad(geo.transpose(0, 2, 1), ((0, 0), (0, 0), (0, 4)))
    geo = jnp.concatenate(pieces(geo), axis=2)
    geo = jnp.pad(geo, ((0, 0), (0, 0), (0, chan - 24)))
    own = jnp.concatenate(
        [
            scalars.reshape(2, slots, chan),
            vectors.reshape(2, slots, 3 * chan),
            geo,
        ],
        axis=2,
    )
    offs = offsets()
    geometry = None
    layers = radial_in.shape[0]
    for layer in range(layers):
        rin = jnp.concatenate(
            [radial_in[layer]]
            + [p[None, :] for p in pieces(radial_bias[layer])]
            + [jnp.zeros((5, hidden), bf16)],
            axis=0,
        )
        rin = (rin * jnp.asarray(0.5, bf16)).T
        weights = [
            rin,
            radial_out[layer].astype(f32),
            atom_in[layer],
            atom_bias[layer][None, :],
            atom_out[layer],
        ]
        last = layer == layers - 1
        if last:
            weights += [readout_in, readout_out[None, :]]
        cols = exchange(own)
        state, extra = layer_call(last, counts, offs, cols, geometry, weights)
        if not last:
            geometry = extra
            own = state.reshape(2, slots, 4 * chan)
    scalar_state = state[:, :chan].reshape(scalars.shape)
    vector_state = state[:, chan:].reshape(vectors.shape)
    every = lax.all_to_all(extra, ("gx", "gy", "gz"), 0, 0, tiled=True)
    energy = jnp.sum(every, axis=0)[:1]
    return scalar_state, vector_state, energy


def solution(mesh):
    in_specs = (
        P("gx", "gy", "gz", None, None),
        P("gx", "gy", "gz"),
        P("gx", "gy", "gz", None, None),
        P("gx", "gy", "gz", None, None, None),
        P(),
        P(),
        P(),
        P(),
        P(),
        P(),
        P(),
        P(),
    )
    out_specs = (P("gx", "gy", "gz", None, None), P("gx", "gy", "gz", None, None, None), P())
    return jax.shard_map(
        on_device, mesh=mesh, in_specs=in_specs, out_specs=out_specs, check_vma=False
    )
```

time: 447 us -> 120 us (0.27)
  local copies, waits for them, and re-layouts: 149 us -> 8.87 us
  matrix products: 67.1 us -> 0 us
  blocking collectives: 63.4 us -> 0 us
  other arithmetic: 58.9 us -> 1.09 us
  starting transfers between devices: 32.9 us -> 70.5 us
  loops' own time: 34.5 us -> 0 us
  waiting for transfers between devices: 37.9 us -> 18.5 us
  Pallas kernels: 0 us -> 18.7 us
    dot_general x131 -> x0, matrix products: 67.1 us -> none  [the longest x32 17.8 us: receiver_block(): lax.dot_general(edge_turned, pair_g, (((1, 2), (0, 1)), ((), ())), prefer...]
    psum x1 -> x0, blocking collectives: 63.4 us -> none  [on_device(): energy = lax.psum(local_energy, ('gx', 'gy', 'gz')).reshape(1)]
    dynamic_slice x108 -> x0, local copies, waits for them, and re-layouts: 41.3 us -> none  [the longest x32 21 us: cell_deltas(): lax.map(one_block, jnp.arange(8, dtype=jnp.int32))]
    reshape x66 -> x3, local copies, waits for them, and re-layouts: 40.3 us -> 0.17 us  [the longest x1 0.1 us: on_device(): positions.reshape(2, 3, slots)]
    another operation x6 -> x0, loops' own time: 34.5 us -> none  [the longest x4 26.3 us: cell_deltas(): lax.map(one_block, jnp.arange(8, dtype=jnp.int32))]
    while x400 -> x0, local copies, waits for them, and re-layouts: 32.5 us -> none
    ppermute x18 -> x20, waiting for transfers between devices: 37.9 us -> 10.1 us  [the longest x16 8.84 us: exchange(): cols.append(lax.ppermute(column, ('gy', 'gz'), pairs))]
    all_to_all x0 -> x1, starting transfers between devices: none -> 20.3 us  [on_device(): every = lax.all_to_all(extra, ('gx', 'gy', 'gz'), 0, 0, tiled=True)]
  transfers between devices with their start and end apart: 18 -> 21, of which waited for: 10 -> 7; matrix products, arithmetic and copies ran while one was open for 2% -> 2% of each run, Pallas kernels for 0% -> 0%
where the time goes in v1:
time: 120 us; the launch traced here: 118 us
  starting transfers between devices  70.5 us (59%)
  Pallas kernels  18.7 us (16%)
  waiting for transfers between devices  18.5 us (15%)
  local copies, waits for them, and re-layouts  8.87 us (7%)
    ppermute x16, starting transfers between devices, exchange(): cols.append(lax.ppermute(column, ('gy', 'gz'), pairs))  29.8 us
    all_to_all x1, starting transfers between devices, on_device(): every = lax.all_to_all(extra, ('gx', 'gy', 'gz'), 0, 0, tiled=True)  20.3 us
    pallas_call x2, Pallas kernels, layer_call(): pl.pallas_call(functools.partial(layer_kernel, last), out_shape=out, in_s...  18.7 us
    ppermute x2, starting transfers between devices, exchange(): low = lax.ppermute(own[1:2], 'gx', up)  10.3 us
    ppermute x2, starting transfers between devices, exchange(): high = lax.ppermute(own[0:1], 'gx', down)  10.1 us
    ppermute x16, waiting for transfers between devices, exchange(): cols.append(lax.ppermute(column, ('gy', 'gz'), pairs))  8.84 us
    all_to_all x1, waiting for transfers between devices, on_device(): every = lax.all_to_all(extra, ('gx', 'gy', 'gz'), 0, 0, tiled=True)  8.42 us
    unnamed x28, local copies, waits for them, and re-layouts  7.68 us
  transfers between devices with their start and end apart: 21, of which 7 were waited for; matrix products, arithmetic and copies ran while one was open for 2% of the time, Pallas kernels for 0%

profile of v1, /device:TPU:1, one launch (start us, length us, event | category | flops | bytes accessed | tf_op | source)
XLA Modules:
  0.0 118.5 jit_solution(13399311483700215873)
XLA Ops:
  0.6 0.6 copy-done
  1.3 0.1 fusion.5
  1.4 0.6 copy-done.9
  2.0 0.1 copy.66
  2.1 0.1 maximum_bitcast_fusion
  2.2 0.8 copy-done.6
  3.1 0.1 fusion.7
  3.2 0.6 copy-done.4
  3.8 2.2 %collective-permute-start = (bf16[1,32,640]{2,1,0:T(8,128)(2,1)S(1)}, bf16[1,32,640]{2,1,0:T(8,128)(2,1)S(1)}, u32[]{:S(2)}, u32[]{:S(2)}) collective-permute-start(bf16[1,32,640]{2,1,0:T(8,128)(2,1)S(1)} %get-tuple-element.33), channel_id=1, source_target_pairs={{0,16},{16,32},{32,48},{48,64},{64,80},{80,96},{96,112},{112,0},{1... | collective-permute-start | bytes 122888 | tf_op jit(solution)/shard_map/ppermute | solution.py:216
  6.0 2.9 %collective-permute-start.1 = (bf16[1,32,640]{2,1,0:T(8,128)(2,1)S(1)}, bf16[1,32,640]{2,1,0:T(8,128)(2,1)S(1)}, u32[]{:S(2)}, u32[]{:S(2)}) collective-permute-start(bf16[1,32,640]{2,1,0:T(8,128)(2,1)S(1)} %get-tuple-element.34), channel_id=1, source_target_pairs={{0,112},{16,0},{32,16},{48,32},{64,48},{80,64},{96,80},{112,96},{1... | collective-permute-start | bytes 122888 | tf_op jit(solution)/shard_map/ppermute | solution.py:217
  9.0 0.7 copy-done.8
  9.6 0.1 stack.5
  9.8 0.9 copy-done.3
  10.6 0.8 copy-done.5
  11.5 0.7 copy-done.11
  12.2 0.1 copy.67
  12.4 5.1 %collective-permute-start.2 = (bf16[4,32,640]{2,1,0:T(8,128)(2,1)S(1)}, bf16[4,32,640]{2,1,0:T(8,128)(2,1)S(1)}, u32[]{:S(2)}, u32[]{:S(2)}) collective-permute-start(bf16[4,32,640]{2,1,0:T(8,128)(2,1)S(1)} %pad_maximum_fusion.refs_4_), channel_id=1, source_target_pairs={{15,0},{12,1},{13,2},{14,3},{3,4},{0,5},{1,6},{2,7},{7,8},{4,9},{5... | collective-permute-start | bytes 491528 | tf_op jit(solution)/shard_map/ppermute | solution.py:231
  17.5 1.4 %collective-permute-start.4 = (bf16[4,32,640]{2,1,0:T(8,128)(2,1)S(1)}, bf16[4,32,640]{2,1,0:T(8,128)(2,1)S(1)}, u32[]{:S(2)}, u32[]{:S(2)}) collective-permute-start(bf16[4,32,640]{2,1,0:T(8,128)(2,1)S(1)} %pad_maximum_fusion.refs_4_), channel_id=1, source_target_pairs={{13,0},{14,1},{15,2},{12,3},{1,4},{2,5},{3,6},{0,7},{5,8},{6,9},{7... | collective-permute-start | bytes 491528 | tf_op jit(solution)/shard_map/ppermute | solution.py:231
  18.9 2.7 %collective-permute-start.6 = (bf16[4,32,640]{2,1,0:T(8,128)(2,1)S(1)}, bf16[4,32,640]{2,1,0:T(8,128)(2,1)S(1)}, u32[]{:S(2)}, u32[]{:S(2)}) collective-permute-start(bf16[4,32,640]{2,1,0:T(8,128)(2,1)S(1)} %pad_maximum_fusion.refs_4_), channel_id=1, source_target_pairs={{1,0},{2,1},{3,2},{0,3},{5,4},{6,5},{7,6},{4,7},{9,8},{10,9},{11,1... | collective-permute-start | bytes 491528 | tf_op jit(solution)/shard_map/ppermute | solution.py:231
  21.6 1.5 %collective-permute-start.7 = (bf16[4,32,640]{2,1,0:T(8,128)(2,1)S(1)}, bf16[4,32,640]{2,1,0:T(8,128)(2,1)S(1)}, u32[]{:S(2)}, u32[]{:S(2)}) collective-permute-start(bf16[4,32,640]{2,1,0:T(8,128)(2,1)S(1)} %pad_maximum_fusion.refs_4_), channel_id=1, source_target_pairs={{7,0},{4,1},{5,2},{6,3},{11,4},{8,5},{9,6},{10,7},{15,8},{12,9},{1... | collective-permute-start | bytes 491528 | tf_op jit(solution)/shard_map/ppermute | solution.py:231
  23.1 0.2 collective-permute-done.3.refs_1_
  23.3 0.4 collective-permute-start.8
  23.6 0.6 collective-permute-done.4.refs_2_
  24.3 4.9 %collective-permute-start.9 = (bf16[4,32,640]{2,1,0:T(8,128)(2,1)S(1)}, bf16[4,32,640]{2,1,0:T(8,128)(2,1)S(1)}, u32[]{:S(2)}, u32[]{:S(2)}) collective-permute-start(bf16[4,32,640]{2,1,0:T(8,128)(2,1)S(1)} %pad_maximum_fusion.refs_4_), channel_id=1, source_target_pairs={{5,0},{6,1},{7,2},{4,3},{9,4},{10,5},{11,6},{8,7},{13,8},{14,9},{1... | collective-permute-start | bytes 491528 | tf_op jit(solution)/shard_map/ppermute | solution.py:231
  29.2 1.3 %collective-permute-done.7.refs_6_ = bf16[4,32,640]{2,1,0:T(8,128)(2,1)S(1)} collective-permute-done((bf16[4,32,640]{2,1,0:T(8,128)(2,1)S(1)}, bf16[4,32,640]{2,1,0:T(8,128)(2,1)S(1)}, u32[]{:S(2)}, u32[]{:S(2)}) %collective-permute-start.7) | collective-permute-done | bytes 163872 | tf_op jit(solution)/shard_map/ppermute | solution.py:231
  30.4 3.0 %collective-permute-done.8.refs_7_ = bf16[4,32,640]{2,1,0:T(8,128)(2,1)S(1)} collective-permute-done((bf16[4,32,640]{2,1,0:T(8,128)(2,1)S(1)}, bf16[4,32,640]{2,1,0:T(8,128)(2,1)S(1)}, u32[]{:S(2)}, u32[]{:S(2)}) %collective-permute-start.8) | collective-permute-done | bytes 163872 | tf_op jit(solution)/shard_map/ppermute | solution.py:231
  33.5 9.0 %layer_first.1 = (bf16[64,512]{1,0:T(8,128)(2,1)S(1)}, f32[72,1152]{1,0:T(8,128)S(1)}) custom-call(s32[2]{0:T(128)S(1)} %bitcast.46, f32[8,1152]{1,0:T(8,128)S(1)} %convert_multiply_fusion.offs_ref, bf16[4,32,640]{2,1,0:T(8,128)(2,1)S(1)} %collective-permute-done.2.refs_0_, bf16[4,32,640]{2,1,0:T(8,128)(2,1)S(1)} %collective-permute-done.3.refs_1_, ...), custom_call_target="tpu_custom_call" | custom-call | tf_op jit(solution)/shard_map/layer_first/pallas_call | solution.py:186
  42.6 8.1 %collective-permute-start.10 = (bf16[1,32,512]{2,1,0:T(8,128)(2,1)S(1)}, bf16[1,32,512]{2,1,0:T(8,128)(2,1)S(1)}, u32[]{:S(2)}, u32[]{:S(2)}) collective-permute-start(bf16[1,32,512]{2,1,0:T(8,128)(2,1)S(1)} %get-tuple-element.37), channel_id=1, source_target_pairs={{0,16},{16,32},{32,48},{48,64},{64,80},{80,96},{96,112},{112,0},{1... | collective-permute-start | bytes 98312 | tf_op jit(solution)/shard_map/ppermute | solution.py:216
  50.7 7.3 %collective-permute-start.11 = (bf16[1,32,512]{2,1,0:T(8,128)(2,1)S(1)}, bf16[1,32,512]{2,1,0:T(8,128)(2,1)S(1)}, u32[]{:S(2)}, u32[]{:S(2)}) collective-permute-start(bf16[1,32,512]{2,1,0:T(8,128)(2,1)S(1)} %get-tuple-element.38), channel_id=1, source_target_pairs={{0,112},{16,0},{32,16},{48,32},{64,48},{80,64},{96,80},{112,96},{1... | collective-permute-start | bytes 98312 | tf_op jit(solution)/shard_map/ppermute | solution.py:217
  58.0 1.2 %collective-permute-done.10 = bf16[1,32,512]{2,1,0:T(8,128)(2,1)S(1)} collective-permute-done((bf16[1,32,512]{2,1,0:T(8,128)(2,1)S(1)}, bf16[1,32,512]{2,1,0:T(8,128)(2,1)S(1)}, u32[]{:S(2)}, u32[]{:S(2)}) %collective-permute-start.10) | collective-permute-done | bytes 32800 | tf_op jit(solution)/shard_map/ppermute | solution.py:216
  59.2 2.3 %collective-permute-start.12 = (bf16[4,32,512]{2,1,0:T(8,128)(2,1)S(1)}, bf16[4,32,512]{2,1,0:T(8,128)(2,1)S(1)}, u32[]{:S(2)}, u32[]{:S(2)}) collective-permute-start(bf16[4,32,512]{2,1,0:T(8,128)(2,1)S(1)} %pad_maximum_fusion.1.refs_4_), channel_id=1, source_target_pairs={{15,0},{12,1},{13,2},{14,3},{3,4},{0,5},{1,6},{2,7},{7,8},{4,9},{5... | collective-permute-start | bytes 393224 | tf_op jit(solution)/shard_map/ppermute | solution.py:231
  61.5 1.7 %collective-permute-start.13 = (bf16[4,32,512]{2,1,0:T(8,128)(2,1)S(1)}, bf16[4,32,512]{2,1,0:T(8,128)(2,1)S(1)}, u32[]{:S(2)}, u32[]{:S(2)}) collective-permute-start(bf16[4,32,512]{2,1,0:T(8,128)(2,1)S(1)} %pad_maximum_fusion.1.refs_4_), channel_id=1, source_target_pairs={{12,0},{13,1},{14,2},{15,3},{0,4},{1,5},{2,6},{3,7},{4,8},{5,9},{6... | collective-permute-start | bytes 393224 | tf_op jit(solution)/shard_map/ppermute | solution.py:231
  63.1 1.3 %collective-permute-start.14 = (bf16[4,32,512]{2,1,0:T(8,128)(2,1)S(1)}, bf16[4,32,512]{2,1,0:T(8,128)(2,1)S(1)}, u32[]{:S(2)}, u32[]{:S(2)}) collective-permute-start(bf16[4,32,512]{2,1,0:T(8,128)(2,1)S(1)} %pad_maximum_fusion.1.refs_4_), channel_id=1, source_target_pairs={{13,0},{14,1},{15,2},{12,3},{1,4},{2,5},{3,6},{0,7},{5,8},{6,9},{7... | collective-permute-start | bytes 393224 | tf_op jit(solution)/shard_map/ppermute | solution.py:231
  64.5 0.1 copy.69
  64.6 0.6 copy-done.7
  65.1 0.1 copy.71.refs_15_
  65.2 0.1 collective-permute-start.15
  65.3 2.9 %collective-permute-start.16 = (bf16[4,32,512]{2,1,0:T(8,128)(2,1)S(1)}, bf16[4,32,512]{2,1,0:T(8,128)(2,1)S(1)}, u32[]{:S(2)}, u32[]{:S(2)}) collective-permute-start(bf16[4,32,512]{2,1,0:T(8,128)(2,1)S(1)} %pad_maximum_fusion.1.refs_4_), channel_id=1, source_target_pairs={{1,0},{2,1},{3,2},{0,3},{5,4},{6,5},{7,6},{4,7},{9,8},{10,9},{11,1... | collective-permute-start | bytes 393224 | tf_op jit(solution)/shard_map/ppermute | solution.py:231
  68.2 1.1 collective-permute-start.18
  69.3 4.5 %collective-permute-start.19 = (bf16[4,32,512]{2,1,0:T(8,128)(2,1)S(1)}, bf16[4,32,512]{2,1,0:T(8,128)(2,1)S(1)}, u32[]{:S(2)}, u32[]{:S(2)}) collective-permute-start(bf16[4,32,512]{2,1,0:T(8,128)(2,1)S(1)} %pad_maximum_fusion.1.refs_4_), channel_id=1, source_target_pairs={{5,0},{6,1},{7,2},{4,3},{9,4},{10,5},{11,6},{8,7},{13,8},{14,9},{1... | collective-permute-start | bytes 393224 | tf_op jit(solution)/shard_map/ppermute | solution.py:231
  73.8 3.7 %collective-permute-done.17.refs_6_ = bf16[4,32,512]{2,1,0:T(8,128)(2,1)S(1)} collective-permute-done((bf16[4,32,512]{2,1,0:T(8,128)(2,1)S(1)}, bf16[4,32,512]{2,1,0:T(8,128)(2,1)S(1)}, u32[]{:S(2)}, u32[]{:S(2)}) %collective-permute-start.17) | collective-permute-done | bytes 131104 | tf_op jit(solution)/shard_map/ppermute | solution.py:231
  77.5 0.7 copy-done.1
  78.2 9.7 %layer_last.1 = (bf16[64,512]{1,0:T(8,128)(2,1)S(1)}, f32[128,128]{1,0:T(8,128)}) custom-call(s32[2]{0:T(128)S(1)} %bitcast.47, f32[8,1152]{1,0:T(8,128)S(1)} %convert_multiply_fusion.offs_ref, bf16[4,32,512]{2,1,0:T(8,128)(2,1)S(1)} %collective-permute-done.12.refs_0_, bf16[4,32,512]{2,1,0:T(8,128)(2,1)S(1)} %collective-permute-done.13.refs_1_, ...), custom_call_target="tpu_custom_call" | custom-call | tf_op jit(solution)/shard_map/layer_last/pallas_call | solution.py:186
  87.9 20.3 %all-to-all-start = ((f32[128,1,128]{2,1,0:T(1,128)}), f32[128,1,128]{2,1,0:T(1,128)S(1)}, u32[]{:S(2)}, u32[]{:S(2)}) async-start(f32[128,1,128]{2,1,0:T(1,128)} %bitcast.21), calls=%async_computation | async-start | bytes 131072 | tf_op jit(solution)/shard_map/all_to_all | solution.py:301
  108.1 0.6 slice.81
  108.8 0.6 copy.74
  109.4 8.4 %all-to-all-done = f32[128,1,128]{2,1,0:T(1,128)S(1)} async-done(((f32[128,1,128]{2,1,0:T(1,128)}), f32[128,1,128]{2,1,0:T(1,128)S(1)}, u32[]{:S(2)}, u32[]{:S(2)}) %all-to-all-start) | async-done | bytes 65568 | tf_op jit(solution)/shard_map/all_to_all | solution.py:301
  117.8 0.7 reduce_sum.9
  (57 shorter events, 0.5 us)
Async XLA Ops:
  0.6 0.7 copy-start
  1.3 0.7 copy-start.9
  2.1 0.8 copy-start.6
  3.0 0.7 copy-start.4
  3.1 6.6 %copy-start.2 = (bf16[2,128,512]{2,1,0:T(8,128)(2,1)S(1)}, bf16[2,128,512]{2,1,0:T(8,128)(2,1)}, u32[]{:S(2)}) copy-start(bf16[2,128,512]{2,1,0:T(8,128)(2,1)} %param.21) | copy-start | bytes 786436
  3.8 8.5 %collective-permute-start = (bf16[1,32,640]{2,1,0:T(8,128)(2,1)S(1)}, bf16[1,32,640]{2,1,0:T(8,128)(2,1)S(1)}, u32[]{:S(2)}, u32[]{:S(2)}) collective-permute-start(bf16[1,32,640]{2,1,0:T(8,128)(2,1)S(1)} %get-tuple-element.33), channel_id=1, source_target_pairs={{0,16},{16,32},{32,48},{48,64},{64,80},{80,96},{96,112},{112,0},{1... | collective-permute-start | bytes 122888 | tf_op jit(solution)/shard_map/ppermute | solution.py:216
  6.0 6.3 %collective-permute-start.1 = (bf16[1,32,640]{2,1,0:T(8,128)(2,1)S(1)}, bf16[1,32,640]{2,1,0:T(8,128)(2,1)S(1)}, u32[]{:S(2)}, u32[]{:S(2)}) collective-permute-start(bf16[1,32,640]{2,1,0:T(8,128)(2,1)S(1)} %get-tuple-element.34), channel_id=1, source_target_pairs={{0,112},{16,0},{32,16},{48,32},{64,48},{80,64},{96,80},{112,96},{1... | collective-permute-start | bytes 122888 | tf_op jit(solution)/shard_map/ppermute | solution.py:217
  8.9 0.7 copy-start.8
  9.7 0.9 copy-start.3
  10.6 0.8 copy-start.5
  11.5 0.7 copy-start.11
  12.3 16.8 %copy-start.10 = (f32[2,128]{1,0:T(2,128)S(1)}, f32[2,128]{1,0:T(2,128)}, u32[]{:S(2)}) copy-start(f32[2,128]{1,0:T(2,128)} %param.20) | copy-start | bytes 3076
  12.4 9.3 %collective-permute-start.2 = (bf16[4,32,640]{2,1,0:T(8,128)(2,1)S(1)}, bf16[4,32,640]{2,1,0:T(8,128)(2,1)S(1)}, u32[]{:S(2)}, u32[]{:S(2)}) collective-permute-start(bf16[4,32,640]{2,1,0:T(8,128)(2,1)S(1)} %pad_maximum_fusion.refs_4_), channel_id=1, source_target_pairs={{15,0},{12,1},{13,2},{14,3},{3,4},{0,5},{1,6},{2,7},{7,8},{4,9},{5... | collective-permute-start | bytes 491528 | tf_op jit(solution)/shard_map/ppermute | solution.py:231
  17.5 5.8 %collective-permute-start.3 = (bf16[4,32,640]{2,1,0:T(8,128)(2,1)S(1)}, bf16[4,32,640]{2,1,0:T(8,128)(2,1)S(1)}, u32[]{:S(2)}, u32[]{:S(2)}) collective-permute-start(bf16[4,32,640]{2,1,0:T(8,128)(2,1)S(1)} %pad_maximum_fusion.refs_4_), channel_id=1, source_target_pairs={{12,0},{13,1},{14,2},{15,3},{0,4},{1,5},{2,6},{3,7},{4,8},{5,9},{6... | collective-permute-start | bytes 491528 | tf_op jit(solution)/shard_map/ppermute | solution.py:231
  17.5 6.8 %collective-permute-start.4 = (bf16[4,32,640]{2,1,0:T(8,128)(2,1)S(1)}, bf16[4,32,640]{2,1,0:T(8,128)(2,1)S(1)}, u32[]{:S(2)}, u32[]{:S(2)}) collective-permute-start(bf16[4,32,640]{2,1,0:T(8,128)(2,1)S(1)} %pad_maximum_fusion.refs_4_), channel_id=1, source_target_pairs={{13,0},{14,1},{15,2},{12,3},{1,4},{2,5},{3,6},{0,7},{5,8},{6,9},{7... | collective-permute-start | bytes 491528 | tf_op jit(solution)/shard_map/ppermute | solution.py:231
  18.9 10.2 %collective-permute-start.5 = (bf16[4,32,640]{2,1,0:T(8,128)(2,1)S(1)}, bf16[4,32,640]{2,1,0:T(8,128)(2,1)S(1)}, u32[]{:S(2)}, u32[]{:S(2)}) collective-permute-start(bf16[4,32,640]{2,1,0:T(8,128)(2,1)S(1)} %pad_maximum_fusion.refs_4_), channel_id=1, source_target_pairs={{3,0},{0,1},{1,2},{2,3},{7,4},{4,5},{5,6},{6,7},{11,8},{8,9},{9,10... | collective-permute-start | bytes 491528 | tf_op jit(solution)/shard_map/ppermute | solution.py:231
  18.9 10.2 %collective-permute-start.6 = (bf16[4,32,640]{2,1,0:T(8,128)(2,1)S(1)}, bf16[4,32,640]{2,1,0:T(8,128)(2,1)S(1)}, u32[]{:S(2)}, u32[]{:S(2)}) collective-permute-start(bf16[4,32,640]{2,1,0:T(8,128)(2,1)S(1)} %pad_maximum_fusion.refs_4_), channel_id=1, source_target_pairs={{1,0},{2,1},{3,2},{0,3},{5,4},{6,5},{7,6},{4,7},{9,8},{10,9},{11,1... | collective-permute-start | bytes 491528 | tf_op jit(solution)/shard_map/ppermute | solution.py:231
  21.6 8.8 %collective-permute-start.7 = (bf16[4,32,640]{2,1,0:T(8,128)(2,1)S(1)}, bf16[4,32,640]{2,1,0:T(8,128)(2,1)S(1)}, u32[]{:S(2)}, u32[]{:S(2)}) collective-permute-start(bf16[4,32,640]{2,1,0:T(8,128)(2,1)S(1)} %pad_maximum_fusion.refs_4_), channel_id=1, source_target_pairs={{7,0},{4,1},{5,2},{6,3},{11,4},{8,5},{9,6},{10,7},{15,8},{12,9},{1... | collective-permute-start | bytes 491528 | tf_op jit(solution)/shard_map/ppermute | solution.py:231
  23.3 10.2 %collective-permute-start.8 = (bf16[4,32,640]{2,1,0:T(8,128)(2,1)S(1)}, bf16[4,32,640]{2,1,0:T(8,128)(2,1)S(1)}, u32[]{:S(2)}, u32[]{:S(2)}) collective-permute-start(bf16[4,32,640]{2,1,0:T(8,128)(2,1)S(1)} %pad_maximum_fusion.refs_4_), channel_id=1, source_target_pairs={{4,0},{5,1},{6,2},{7,3},{8,4},{9,5},{10,6},{11,7},{12,8},{13,9},{1... | collective-permute-start | bytes 491528 | tf_op jit(solution)/shard_map/ppermute | solution.py:231
  24.3 9.2 %collective-permute-start.9 = (bf16[4,32,640]{2,1,0:T(8,128)(2,1)S(1)}, bf16[4,32,640]{2,1,0:T(8,128)(2,1)S(1)}, u32[]{:S(2)}, u32[]{:S(2)}) collective-permute-start(bf16[4,32,640]{2,1,0:T(8,128)(2,1)S(1)} %pad_maximum_fusion.refs_4_), channel_id=1, source_target_pairs={{5,0},{6,1},{7,2},{4,3},{9,4},{10,5},{11,6},{8,7},{13,8},{14,9},{1... | collective-permute-start | bytes 491528 | tf_op jit(solution)/shard_map/ppermute | solution.py:231
  42.6 16.6 %collective-permute-start.10 = (bf16[1,32,512]{2,1,0:T(8,128)(2,1)S(1)}, bf16[1,32,512]{2,1,0:T(8,128)(2,1)S(1)}, u32[]{:S(2)}, u32[]{:S(2)}) collective-permute-start(bf16[1,32,512]{2,1,0:T(8,128)(2,1)S(1)} %get-tuple-element.37), channel_id=1, source_target_pairs={{0,16},{16,32},{32,48},{48,64},{64,80},{80,96},{96,112},{112,0},{1... | collective-permute-start | bytes 98312 | tf_op jit(solution)/shard_map/ppermute | solution.py:216
  50.7 8.5 %collective-permute-start.11 = (bf16[1,32,512]{2,1,0:T(8,128)(2,1)S(1)}, bf16[1,32,512]{2,1,0:T(8,128)(2,1)S(1)}, u32[]{:S(2)}, u32[]{:S(2)}) collective-permute-start(bf16[1,32,512]{2,1,0:T(8,128)(2,1)S(1)} %get-tuple-element.38), channel_id=1, source_target_pairs={{0,112},{16,0},{32,16},{48,32},{64,48},{80,64},{96,80},{112,96},{1... | collective-permute-start | bytes 98312 | tf_op jit(solution)/shard_map/ppermute | solution.py:217
  59.2 9.0 %collective-permute-start.12 = (bf16[4,32,512]{2,1,0:T(8,128)(2,1)S(1)}, bf16[4,32,512]{2,1,0:T(8,128)(2,1)S(1)}, u32[]{:S(2)}, u32[]{:S(2)}) collective-permute-start(bf16[4,32,512]{2,1,0:T(8,128)(2,1)S(1)} %pad_maximum_fusion.1.refs_4_), channel_id=1, source_target_pairs={{15,0},{12,1},{13,2},{14,3},{3,4},{0,5},{1,6},{2,7},{7,8},{4,9},{5... | collective-permute-start | bytes 393224 | tf_op jit(solution)/shard_map/ppermute | solution.py:231
  61.5 6.7 %collective-permute-start.13 = (bf16[4,32,512]{2,1,0:T(8,128)(2,1)S(1)}, bf16[4,32,512]{2,1,0:T(8,128)(2,1)S(1)}, u32[]{:S(2)}, u32[]{:S(2)}) collective-permute-start(bf16[4,32,512]{2,1,0:T(8,128)(2,1)S(1)} %pad_maximum_fusion.1.refs_4_), channel_id=1, source_target_pairs={{12,0},{13,1},{14,2},{15,3},{0,4},{1,5},{2,6},{3,7},{4,8},{5,9},{6... | collective-permute-start | bytes 393224 | tf_op jit(solution)/shard_map/ppermute | solution.py:231
  63.1 6.2 %collective-permute-start.14 = (bf16[4,32,512]{2,1,0:T(8,128)(2,1)S(1)}, bf16[4,32,512]{2,1,0:T(8,128)(2,1)S(1)}, u32[]{:S(2)}, u32[]{:S(2)}) collective-permute-start(bf16[4,32,512]{2,1,0:T(8,128)(2,1)S(1)} %pad_maximum_fusion.1.refs_4_), channel_id=1, source_target_pairs={{13,0},{14,1},{15,2},{12,3},{1,4},{2,5},{3,6},{0,7},{5,8},{6,9},{7... | collective-permute-start | bytes 393224 | tf_op jit(solution)/shard_map/ppermute | solution.py:231
  64.4 0.7 copy-start.7
  65.2 8.6 %collective-permute-start.15 = (bf16[4,32,512]{2,1,0:T(8,128)(2,1)S(1)}, bf16[4,32,512]{2,1,0:T(8,128)(2,1)S(1)}, u32[]{:S(2)}, u32[]{:S(2)}) collective-permute-start(bf16[4,32,512]{2,1,0:T(8,128)(2,1)S(1)} %pad_maximum_fusion.1.refs_4_), channel_id=1, source_target_pairs={{3,0},{0,1},{1,2},{2,3},{7,4},{4,5},{5,6},{6,7},{11,8},{8,9},{9,10... | collective-permute-start | bytes 393224 | tf_op jit(solution)/shard_map/ppermute | solution.py:231
  65.3 8.5 %collective-permute-start.16 = (bf16[4,32,512]{2,1,0:T(8,128)(2,1)S(1)}, bf16[4,32,512]{2,1,0:T(8,128)(2,1)S(1)}, u32[]{:S(2)}, u32[]{:S(2)}) collective-permute-start(bf16[4,32,512]{2,1,0:T(8,128)(2,1)S(1)} %pad_maximum_fusion.1.refs_4_), channel_id=1, source_target_pairs={{1,0},{2,1},{3,2},{0,3},{5,4},{6,5},{7,6},{4,7},{9,8},{10,9},{11,1... | collective-permute-start | bytes 393224 | tf_op jit(solution)/shard_map/ppermute | solution.py:231
  68.2 9.3 %collective-permute-start.17 = (bf16[4,32,512]{2,1,0:T(8,128)(2,1)S(1)}, bf16[4,32,512]{2,1,0:T(8,128)(2,1)S(1)}, u32[]{:S(2)}, u32[]{:S(2)}) collective-permute-start(bf16[4,32,512]{2,1,0:T(8,128)(2,1)S(1)} %pad_maximum_fusion.1.refs_4_), channel_id=1, source_target_pairs={{7,0},{4,1},{5,2},{6,3},{11,4},{8,5},{9,6},{10,7},{15,8},{12,9},{1... | collective-permute-start | bytes 393224 | tf_op jit(solution)/shard_map/ppermute | solution.py:231
  68.2 9.3 %collective-permute-start.18 = (bf16[4,32,512]{2,1,0:T(8,128)(2,1)S(1)}, bf16[4,32,512]{2,1,0:T(8,128)(2,1)S(1)}, u32[]{:S(2)}, u32[]{:S(2)}) collective-permute-start(bf16[4,32,512]{2,1,0:T(8,128)(2,1)S(1)} %pad_maximum_fusion.1.refs_4_), channel_id=1, source_target_pairs={{4,0},{5,1},{6,2},{7,3},{8,4},{9,5},{10,6},{11,7},{12,8},{13,9},{1... | collective-permute-start | bytes 393224 | tf_op jit(solution)/shard_map/ppermute | solution.py:231
  69.3 8.2 %collective-permute-start.19 = (bf16[4,32,512]{2,1,0:T(8,128)(2,1)S(1)}, bf16[4,32,512]{2,1,0:T(8,128)(2,1)S(1)}, u32[]{:S(2)}, u32[]{:S(2)}) collective-permute-start(bf16[4,32,512]{2,1,0:T(8,128)(2,1)S(1)} %pad_maximum_fusion.1.refs_4_), channel_id=1, source_target_pairs={{5,0},{6,1},{7,2},{4,3},{9,4},{10,5},{11,6},{8,7},{13,8},{14,9},{1... | collective-permute-start | bytes 393224 | tf_op jit(solution)/shard_map/ppermute | solution.py:231
  77.5 0.7 copy-start.1
  87.9 30.0 %all-to-all-start = ((f32[128,1,128]{2,1,0:T(1,128)}), f32[128,1,128]{2,1,0:T(1,128)S(1)}, u32[]{:S(2)}, u32[]{:S(2)}) async-start(f32[128,1,128]{2,1,0:T(1,128)} %bitcast.21), calls=%async_computation | async-start | bytes 131072 | tf_op jit(solution)/shard_map/all_to_all | solution.py:301

commit v2 on v1

v2 whole, which is shorter than its diff:
```python
import functools
import math

import jax
import jax.numpy as jnp
from jax import lax
from jax.experimental import pallas as pl
from jax.experimental.pallas import tpu as pltpu
from jax.sharding import PartitionSpec as P

cutoff = 5.0
message_scale = 0.5
slots = 32
chan = 128
hidden = 64
block = 4
blocks = slots // block
own_atoms, own_main, own_span = 576, 512, 640
side_atoms, side_main, side_span = 288, 256, 384
f32 = jnp.float32
bf16 = jnp.bfloat16
across = (((1,), (1,)), ((), ()))


def pieces(value):
    high = lax.reduce_precision(value, 8, 7)
    rest = value - high
    middle = lax.reduce_precision(rest, 8, 7)
    low = lax.reduce_precision(rest - middle, 8, 7)
    return high.astype(bf16), middle.astype(bf16), low.astype(bf16)


def dot(a, b):
    return jnp.dot(a, b, preferred_element_type=f32)


def half_silu(y):
    return y + y * jnp.tanh(y)


def iotas(shape):
    return lax.broadcasted_iota(jnp.int32, shape, 0), lax.broadcasted_iota(jnp.int32, shape, 1)


def flag(condition):
    return jnp.where(condition, 1.0, 0.0)


def rows_of(geo):
    row, lane = iotas((8, chan))
    pick = flag((lane == row) | (lane == row + 8) | (lane == row + 16)).astype(bf16)
    return lax.dot_general(pick, geo, across, preferred_element_type=f32)


def columns_of(geo):
    row, lane = iotas((chan, chan))
    pick = flag((lane == row) | (lane + 8 == row) | (lane + 16 == row)).astype(bf16)
    return dot(geo, pick)


def compaction(live, span):
    atoms = live.shape[1]
    row, lane = iotas((atoms, atoms))
    before = flag(row < lane).astype(bf16)
    rank = dot(jnp.broadcast_to(live, (8, atoms)).astype(bf16), before)[0:1]
    rank = jnp.where(live > 0.5, rank, -1.0)
    row = lax.broadcasted_iota(jnp.int32, (span, atoms), 0).astype(f32)
    return flag(row == rank).astype(bf16)


def geometry(q, row, mine, shift, basis_ref, wts_ref, at):
    dist2 = None
    disp = []
    for k in range(3):
        other = row[k : k + 1] + (row[4 + k : 5 + k] + (shift if k == 0 else 0.0))
        d = other - mine[:, k : k + 1]
        disp.append(d)
        dist2 = d * d if k == 0 else dist2 + d * d
    live = row[3:4]
    number = lax.broadcasted_iota(jnp.int32, dist2.shape, 0) + (q * slots + 1)
    itself = flag(row[7:8] == number.astype(f32))
    dist = jnp.sqrt(dist2 + itself + (1.0 - live))
    smooth = jnp.where(dist < cutoff, 0.5 * (jnp.cos(math.pi * dist / cutoff) + 1.0), 0.0)
    weight = smooth * live * (1.0 - itself)
    scaled = weight / dist
    wts_ref[at, 0, :] = weight
    for k in range(3):
        wts_ref[at, 1 + k, :] = scaled * disp[k]
    sharp = 0.5 * (7.0 / cutoff) ** 2
    for k in range(8):
        away = dist - k * (cutoff / 7.0)
        basis_ref[at, k, :] = jnp.exp(-sharp * (away * away))


def features(layer, x, part, weights, feats):
    _, _, ain_ref, abias_ref, aout_ref = weights
    s = x[:, :chan]
    bias = abias_ref[layer : layer + 1, :]
    hid = half_silu(0.5 * (dot(s, ain_ref[layer]) + bias)).astype(bf16)
    gates = dot(hid, aout_ref[layer]).astype(bf16)
    ga, gb = gates[:, :chan], gates[:, chan : 2 * chan]
    gc, gg = gates[:, 2 * chan : 3 * chan], gates[:, 3 * chan :]
    vec = [x[:, (k + 1) * chan : (k + 2) * chan] for k in range(3)]
    feats[0][part, :] = jnp.concatenate([ga] + [gb * v for v in vec], axis=1)
    for k in range(3):
        feats[1 + k][part, :] = jnp.concatenate([gc, gg * vec[k]], axis=1)


def messages(layer, q, count, window, weights, basis_ref, wts_ref, feats, edges, delta):
    rin_ref, rout_ref = weights[:2]
    width = window.stop - window.start

    def one_block(b, carry):
        for r in range(block):
            i = q * slots + b * block + r
            wide = jnp.concatenate(
                [basis_ref[i][:, window], jnp.ones((8, width), f32)], axis=0
            ).astype(bf16)
            s = half_silu(dot(rin_ref[layer], wide)).astype(bf16).reshape(4, 16, width)
            part = slice(r * hidden, (r + 1) * hidden)
            w = wts_ref[i][:, window]
            for g in range(4):
                line = jnp.broadcast_to(w[g : g + 1, :], (16, width)).astype(bf16)
                edges[g][part, :width] = (s * line[None]).reshape(hidden, width)
        plain = dot(edges[0][:, :width], feats[0][window, :])
        turned = [dot(edges[k + 1][:, :width], feats[k + 1][window, :]) for k in range(3)]
        radial = [rout_ref[layer, :, g * chan : (g + 1) * chan].astype(f32)[None] for g in range(4)]
        split = (block, hidden, chan)
        proj = turned[0][:, chan:] + turned[1][:, chan:] + turned[2][:, chan:]
        totals = [plain[:, :chan].reshape(split) * radial[0] + proj.reshape(split) * radial[3]]
        for k in range(3):
            totals.append(
                plain[:, (k + 1) * chan : (k + 2) * chan].reshape(split) * radial[1]
                + turned[k][:, :chan].reshape(split) * radial[2]
            )
        at = q * blocks + b
        for g in range(4):
            lanes = slice(g * chan, (g + 1) * chan)
            delta[at, 0:block, lanes] += jnp.sum(totals[g], axis=1)
        return carry

    lax.fori_loop(0, (count + block - 1) // block, one_block, 0)


def own_kernel(layer, *refs):
    counts_ref, low, middle, high = refs[:4]
    weights = refs[4:9]
    refs = refs[9:]
    if layer == 0:
        table_ref, delta, basis, wts, order, more = refs[:6]
        refs = refs[6:]
    else:
        basis, wts, order, more, delta = refs[:5]
        refs = refs[5:]
    feats, edges = refs[:4], refs[4:8]
    parts = [ref[...].reshape(own_atoms // 3, -1) for ref in (low, middle, high)]
    third = own_atoms // 3
    if layer == 0:
        geo = jnp.concatenate([p[:, 4 * chan :] for p in parts], axis=0) + table_ref[...]
        live = rows_of(geo)[3:4]
        order[...] = compaction(live, own_span)
        row = rows_of(dot(order[...], geo).astype(bf16))
        total = jnp.sum(live)
        more[0] = jnp.where(total > own_main + 0.5, 1, 0)
        for q in range(2):
            mine = columns_of(middle[q, 1][:, 4 * chan :])
            at = slice(q * slots, (q + 1) * slots)
            geometry(q, row, mine, -q * cutoff, basis, wts, at)

    def gathered(part):
        x = None
        for n in range(3):
            y = dot(order[part, n * third : (n + 1) * third], parts[n][:, : 4 * chan])
            x = y if n == 0 else x + y
        features(layer, x.astype(bf16), part, weights, feats)

    delta[...] = jnp.zeros_like(delta)
    main, rest = slice(0, own_main), slice(own_main, own_span)
    gathered(main)
    for q in range(2):
        messages(layer, q, counts_ref[q], main, weights, basis, wts, feats, edges, delta)

    @pl.when(more[0] > 0)
    def _():
        gathered(rest)
        for q in range(2):
            messages(layer, q, counts_ref[q], rest, weights, basis, wts, feats, edges, delta)


def side_kernel(layer, last, *refs):
    counts_ref, low, high, own_ref, before = refs[:5]
    weights = refs[5:10]
    refs = refs[10:]
    if last:
        read_in_ref, read_out_ref = refs[:2]
        refs = refs[2:]
    if layer == 0:
        table_ref, refs = refs[0], refs[1:]
    else:
        (basis, wts, order, more), refs = refs[:4], refs[4:]
    state_ref, refs = refs[0], refs[1:]
    if last:
        energy_ref, refs = refs[0], refs[1:]
    if layer == 0:
        (basis, wts, order, more), refs = refs[:4], refs[4:]
    feats, edges, delta = refs[:4], refs[4:8], refs[8]
    delta[...] = before[...]
    main, rest = slice(0, side_main), slice(side_main, side_span)
    for q in range(2):
        x_all = (low, high)[q][...].reshape(side_atoms, -1)
        if layer == 0:
            geo = x_all[:, 4 * chan :] + table_ref[...]
            live = rows_of(geo)[3:4]
            order[q] = compaction(live, side_span)
            row = rows_of(dot(order[q], geo).astype(bf16))
            total = jnp.sum(live)
            more[q] = jnp.where(total > side_main + 0.5, 1, 0)
            mine = columns_of(own_ref[q][:, 4 * chan :])
            at = slice(q * slots, (q + 1) * slots)
            geometry(q, row, mine, (-cutoff, cutoff)[q], basis, wts, at)

        def gathered(part, q=q, x_all=x_all):
            x = dot(order[q, part, :], x_all[:, : 4 * chan])
            features(layer, x.astype(bf16), part, weights, feats)

        gathered(main)
        messages(layer, q, counts_ref[q], main, weights, basis, wts, feats, edges, delta)

        @pl.when(more[q] > 0)
        def _(q=q, gathered=gathered):
            gathered(rest)
            messages(layer, q, counts_ref[q], rest, weights, basis, wts, feats, edges, delta)

    slot = lax.broadcasted_iota(jnp.int32, (2 * slots, 1), 0)
    limit = jnp.where(slot < slots, counts_ref[0], counts_ref[1] + slots)
    live = flag(slot < limit)
    mine = own_ref[...].reshape(2 * slots, -1)[:, : 4 * chan].astype(f32)
    change = jnp.concatenate([delta[b, 0:block, :] for b in range(2 * blocks)], axis=0)
    state = ((mine + message_scale * change) * live).astype(bf16)
    state_ref[...] = state
    if last:
        x = dot(state[:, :chan], read_in_ref[...])
        each = half_silu(0.5 * x) * read_out_ref[...] * live
        energy_ref[...] = jnp.broadcast_to(jnp.sum(each, keepdims=True), energy_ref.shape)


vmem = pl.BlockSpec(memory_space=pltpu.VMEM)
smem = pl.BlockSpec(memory_space=pltpu.SMEM)


def scratch(span, main):
    return [
        pltpu.VMEM((span, 4 * chan), bf16),
        *[pltpu.VMEM((span, 2 * chan), bf16)] * 3,
        *[pltpu.VMEM((block * hidden, main), bf16)] * 4,
    ]


def cost(atoms):
    return pl.CostEstimate(
        flops=2 * 2 * slots * atoms * 81920, bytes_accessed=4000000, transcendentals=4000000
    )


params = pltpu.CompilerParams(vmem_limit_bytes=40 * 1024 * 1024)
delta_shape = jax.ShapeDtypeStruct((2 * blocks, 8, 4 * chan), f32)


def kept_shapes(span, order):
    pairs = jax.ShapeDtypeStruct((2 * slots, 8, span), f32)
    return (
        pairs,
        pairs,
        jax.ShapeDtypeStruct(order, bf16),
        jax.ShapeDtypeStruct((2,), jnp.int32),
    )


kept_specs = (vmem, vmem, vmem, smem)


def own_call(layer, counts, ys, weights, table, kept):
    operands = [counts, *ys, *weights]
    specs = [smem] + [vmem] * (len(operands) - 1)
    shapes, outs = (delta_shape,), (vmem,)
    if layer == 0:
        operands.append(table)
        specs.append(vmem)
        shapes += kept_shapes(own_span, (own_span, own_atoms))
        outs += kept_specs
    else:
        operands += kept
        specs += kept_specs
    return pl.pallas_call(
        functools.partial(own_kernel, layer),
        out_shape=shapes,
        in_specs=specs,
        out_specs=outs,
        scratch_shapes=scratch(own_span, own_main),
        compiler_params=params,
        cost_estimate=cost(own_atoms),
        name=f"own_part_{layer}",
    )(*operands)


def side_call(layer, last, counts, low, high, own, delta, weights, readout, table, kept):
    operands = [counts, low, high, own, delta, *weights]
    specs = [smem] + [vmem] * (len(operands) - 1)
    shapes, outs = (jax.ShapeDtypeStruct((2 * slots, 4 * chan), bf16),), (vmem,)
    if last:
        operands += readout
        specs += [vmem] * 2
        shapes += (jax.ShapeDtypeStruct((chan, chan), f32),)
        outs += (vmem,)
    if layer == 0:
        operands.append(table)
        specs.append(vmem)
        shapes += kept_shapes(side_span, (2, side_span, side_atoms))
        outs += kept_specs
    else:
        operands += kept
        specs += kept_specs
    return pl.pallas_call(
        functools.partial(side_kernel, layer, last),
        out_shape=shapes,
        in_specs=specs,
        out_specs=outs,
        scratch_shapes=scratch(side_span, side_main) + [pltpu.VMEM(delta_shape.shape, f32)],
        compiler_params=params,
        cost_estimate=cost(side_atoms),
        name=f"side_part_{layer}",
    )(*operands)


def shifted(value, axis, step):
    count = lax.axis_size(axis)
    return lax.ppermute(value, axis, [((i + step) % count, i) for i in range(count)])


def tables():
    j = lax.broadcasted_iota(jnp.int32, (own_atoms, chan), 0)
    lane = lax.broadcasted_iota(jnp.int32, (own_atoms, chan), 1)
    slot, z, plane, y = j % slots, j // slots % 3, j // (3 * slots) % 2, j // (6 * slots)
    name = jnp.where((y == 1) & (z == 1), plane * slots + slot + 1, 0)
    values = jnp.where(lane == 4, plane * 5, 0) + jnp.where(lane == 7, name, 0)
    values += jnp.where(lane == 5, (y - 1) * 5, 0) + jnp.where(lane == 6, (z - 1) * 5, 0)
    own = values.astype(bf16)
    j, lane = j[:side_atoms], lane[:side_atoms]
    z, y = j // slots % 3, j // (3 * slots)
    values = jnp.where(lane == 5, (y - 1) * 5, 0) + jnp.where(lane == 6, (z - 1) * 5, 0)
    return own, values.astype(bf16)


def on_device(
    positions,
    counts,
    scalars,
    vectors,
    radial_in,
    radial_bias,
    radial_out,
    atom_in,
    atom_bias,
    atom_out,
    readout_in,
    readout_out,
):
    counts = counts.reshape(2)
    live = (lax.broadcasted_iota(jnp.int32, (2, slots), 1) < counts[:, None]).astype(f32)
    geo = jnp.concatenate([positions.reshape(2, 3, slots), live[:, None, :]], axis=1)
    geo = jnp.pad(geo.transpose(0, 2, 1), ((0, 0), (0, 0), (0, 4)))
    geo = jnp.concatenate(pieces(geo), axis=2)
    geo = jnp.pad(geo, ((0, 0), (0, 0), (0, chan - 24)))
    own = jnp.concatenate(
        [
            scalars.reshape(2, slots, chan),
            vectors.reshape(2, slots, 3 * chan),
            geo,
        ],
        axis=2,
    )
    layers = radial_in.shape[0]
    rin = jnp.concatenate(
        [radial_in]
        + [p[:, None, :] for p in pieces(radial_bias)]
        + [jnp.zeros((layers, 5, hidden), bf16)],
        axis=1,
    )
    rin = (rin * jnp.asarray(0.5, bf16)).transpose(0, 2, 1)
    weights = [rin, radial_out, atom_in, atom_bias, atom_out]
    own_table, side_table = tables()
    own_kept = side_kept = ()
    for layer in range(layers):
        last = layer == layers - 1
        y = jnp.stack([shifted(own, "gz", -1), own, shifted(own, "gz", 1)], axis=1)
        ys = [shifted(y, "gy", -1), y, shifted(y, "gy", 1)]
        low = shifted(jnp.stack([v[1] for v in ys]), "gx", -1)
        high = shifted(jnp.stack([v[0] for v in ys]), "gx", 1)
        delta, *kept = own_call(layer, counts, ys, weights, own_table, own_kept)
        own_kept = own_kept or kept
        readout = [readout_in, readout_out[None, :]]
        state, *kept = side_call(
            layer, last, counts, low, high, own, delta, weights, readout, side_table, side_kept
        )
        if last:
            energy = kept[0]
        else:
            side_kept = side_kept or kept
            own = state.reshape(2, slots, 4 * chan)
    scalar_state = state[:, :chan].reshape(scalars.shape)
    vector_state = state[:, chan:].reshape(vectors.shape)
    every = lax.all_to_all(energy, ("gx", "gy", "gz"), 0, 0, tiled=True)
    energy = jnp.sum(every, axis=0)[:1]
    return scalar_state, vector_state, energy


def solution(mesh):
    in_specs = (
        P("gx", "gy", "gz", None, None),
        P("gx", "gy", "gz"),
        P("gx", "gy", "gz", None, None),
        P("gx", "gy", "gz", None, None, None),
        P(),
        P(),
        P(),
        P(),
        P(),
        P(),
        P(),
        P(),
    )
    out_specs = (P("gx", "gy", "gz", None, None), P("gx", "gy", "gz", None, None, None), P())
    return jax.shard_map(
        on_device, mesh=mesh, in_specs=in_specs, out_specs=out_specs, check_vma=False
    )
```

time: 120 us -> 120 us (level)
  starting transfers between devices: 70.5 us -> 52.9 us
  waiting for transfers between devices: 18.5 us -> 36.1 us
  other arithmetic: 1.09 us -> 4.88 us
  local copies, waits for them, and re-layouts: 8.87 us -> 5.85 us
    ppermute x20 -> x12, waiting for transfers between devices: 10.1 us -> 27.7 us  [shifted(): lax.ppermute(value, axis, [((i + step) % count, i) for i in range(count)])]
    ppermute x20 -> x12, starting transfers between devices: 50.2 us -> 37.4 us  [shifted(): lax.ppermute(value, axis, [((i + step) % count, i) for i in range(count)])]
    all_to_all x1, starting transfers between devices: 20.3 us -> 15.5 us  [on_device(): every = lax.all_to_all(energy, ('gx', 'gy', 'gz'), 0, 0, tiled=True)]
    unnamed x28 -> x31, local copies, waits for them, and re-layouts: 7.68 us -> 4.24 us
    convert_element_type x1 -> x2, other arithmetic: 0.02 us -> 1.56 us  [the longest x1 1.26 us: tables(): own = values.astype(bf16)]
    pallas_call x2 -> x4, Pallas kernels: 18.7 us -> 17.6 us  [the longest x2 8.97 us: own_call(): pl.pallas_call(functools.partial(own_kernel, layer), out_shape=shapes, in...]
  transfers between devices with their start and end apart: 21 -> 13, of which waited for: 7 -> 10; matrix products, arithmetic and copies ran while one was open for 2% -> 5% of each run, Pallas kernels for 0% -> 8%
where the time goes in v2:
time: 120 us; the launch traced here: 118 us
  starting transfers between devices  52.9 us (44%)
  waiting for transfers between devices  36.1 us (30%)
  Pallas kernels  17.6 us (15%)
  local copies, waits for them, and re-layouts  5.85 us (5%)
  other arithmetic  4.88 us (4%)
    ppermute x12, starting transfers between devices, shifted(): lax.ppermute(value, axis, [((i + step) % count, i) for i in range(count)])  37.4 us
    ppermute x12, waiting for transfers between devices, shifted(): lax.ppermute(value, axis, [((i + step) % count, i) for i in range(count)])  27.7 us
    all_to_all x1, starting transfers between devices, on_device(): every = lax.all_to_all(energy, ('gx', 'gy', 'gz'), 0, 0, tiled=True)  15.5 us
    pallas_call x2, Pallas kernels, own_call(): pl.pallas_call(functools.partial(own_kernel, layer), out_shape=shapes, in...  8.97 us
    pallas_call x2, Pallas kernels, side_call(): pl.pallas_call(functools.partial(side_kernel, layer, last), out_shape=sha...  8.68 us
    all_to_all x1, waiting for transfers between devices, on_device(): every = lax.all_to_all(energy, ('gx', 'gy', 'gz'), 0, 0, tiled=True)  8.42 us
    unnamed x31, local copies, waits for them, and re-layouts  4.24 us
  transfers between devices with their start and end apart: 13, of which 10 were waited for; matrix products, arithmetic and copies ran while one was open for 5% of the time, Pallas kernels for 8%

profile of v2, /device:TPU:1, one launch (start us, length us, event | category | flops | bytes accessed | tf_op | source)
XLA Modules:
  0.0 118.4 jit_solution(11595631686144826049)
XLA Ops:
  0.6 0.7 fusion.24
  1.4 0.7 copy.138
  2.0 0.1 copy.118
  2.1 0.1 maximum_bitcast_fusion
  2.2 0.8 copy.116
  3.1 0.1 reshape.70
  3.1 0.1 fusion.26
  3.2 0.7 fusion.45
  4.0 2.1 %collective-permute-start = (bf16[2,32,640]{2,1,0:T(8,128)(2,1)S(1)}, bf16[2,32,640]{2,1,0:T(8,128)(2,1)S(1)}, u32[]{:S(2)}, u32[]{:S(2)}) collective-permute-start(bf16[2,32,640]{2,1,0:T(8,128)(2,1)S(1)} %get-tuple-element.62.refs_3_), channel_id=1, source_target_pairs={{3,0},{0,1},{1,2},{2,3},{7,4},{4,5},{5,6},{6,7},{11,8},{8,9},{9,10... | collective-permute-start | bytes 245768 | tf_op jit(solution)/shard_map/ppermute | solution.py:337
  6.1 1.3 %collective-permute-start.1 = (bf16[2,32,640]{2,1,0:T(8,128)(2,1)S(1)}, bf16[2,32,640]{2,1,0:T(8,128)(2,1)S(1)}, u32[]{:S(2)}, u32[]{:S(2)}) collective-permute-start(bf16[2,32,640]{2,1,0:T(8,128)(2,1)S(1)} %get-tuple-element.62.refs_3_), channel_id=1, source_target_pairs={{1,0},{2,1},{3,2},{0,3},{5,4},{6,5},{7,6},{4,7},{9,8},{10,9},{11,1... | collective-permute-start | bytes 245768 | tf_op jit(solution)/shard_map/ppermute | solution.py:337
  7.6 0.3 fusion.15.refs_10_
  7.9 1.3 %fusion.4.refs_9_ = bf16[576,128]{1,0:T(8,128)(2,1)S(1)} fusion(s32[576]{0:T(1024)S(1)} %get-tuple-element.72, s32[576]{0:T(1024)S(1)} %get-tuple-element.75, s32[576]{0:T(1024)S(1)} %get-tuple-element.71, s32[576]{0:T(1024)S(1)} %get-tuple-element.76, s32[576]{0:T(1024)S(1)} %get-tuple-element.73, s32[576]{0:T(1024)S(1)} %get-tuple-element.81, ...), kind=kLoop, calls=%fused_computation.14 | loop fusion | flops 3022848 | bytes 168704 | tf_op jit(solution)/shard_map/convert_element_type | solution.py:347
  9.1 0.7 fusion.43
  9.8 0.1 copy.120
  9.9 0.1 copy.121
  10.1 0.1 copy.122
  10.2 0.8 copy.119
  11.0 0.1 concatenate.15
  11.2 4.9 %collective-permute-start.2 = (bf16[2,3,32,640]{3,2,0,1:T(8,128)(2,1)S(1)}, bf16[2,3,32,640]{3,2,0,1:T(8,128)(2,1)S(1)}, u32[]{:S(2)}, u32[]{:S(2)}) collective-permute-start(bf16[2,3,32,640]{3,2,0,1:T(8,128)(2,1)S(1)} %pad_maximum_fusion.4), channel_id=1, source_target_pairs={{12,0},{0,4},{4,8},{8,12},{13,1},{1,5},{5,9},{9,13},{14,2},{2,6},{... | collective-permute-start | bytes 737288 | tf_op jit(solution)/shard_map/ppermute | solution.py:337
  16.2 5.7 %collective-permute-done.2 = bf16[2,3,32,640]{3,2,0,1:T(8,128)(2,1)S(1)} collective-permute-done((bf16[2,3,32,640]{3,2,0,1:T(8,128)(2,1)S(1)}, bf16[2,3,32,640]{3,2,0,1:T(8,128)(2,1)S(1)}, u32[]{:S(2)}, u32[]{:S(2)}) %collective-permute-start.2) | collective-permute-done | bytes 245792 | tf_op jit(solution)/shard_map/ppermute | solution.py:337
  21.9 1.4 %collective-permute-done.3 = bf16[2,3,32,640]{3,2,0,1:T(8,128)(2,1)S(1)} collective-permute-done((bf16[2,3,32,640]{3,2,0,1:T(8,128)(2,1)S(1)}, bf16[2,3,32,640]{3,2,0,1:T(8,128)(2,1)S(1)}, u32[]{:S(2)}, u32[]{:S(2)}) %collective-permute-start.3) | collective-permute-done | bytes 245792 | tf_op jit(solution)/shard_map/ppermute | solution.py:337
  23.3 0.1 pad_maximum_fusion.1
  23.4 3.3 %collective-permute-start.5 = (bf16[3,3,32,640]{3,2,0,1:T(8,128)(2,1)S(1)}, bf16[3,3,32,640]{3,2,0,1:T(8,128)(2,1)S(1)}, u32[]{:S(2)}, u32[]{:S(2)}) collective-permute-start(bf16[3,3,32,640]{3,2,0,1:T(8,128)(2,1)S(1)} %pad_maximum_fusion.1), channel_id=1, source_target_pairs={{16,0},{32,16},{48,32},{64,48},{80,64},{96,80},{112,96},{0,112},{1... | collective-permute-start | bytes 1105928 | tf_op jit(solution)/shard_map/ppermute | solution.py:337
  26.6 0.1 pad_maximum_fusion
  26.7 0.1 collective-permute-start.4
  26.9 6.1 %own_part_0.1 = (f32[16,8,512]{2,1,0:T(8,128)S(1)}, f32[64,8,640]{2,1,0:T(8,128)S(1)}, f32[64,8,640]{2,1,0:T(8,128)S(1)}, bf16[640,576]{1,0:T(8,128)(2,1)S(1)}, s32[2]{0:T(128)S(1)}) custom-call(s32[2]{0:T(128)S(1)} %bitcast.38, bf16[2,3,32,640]{3,2,1,0:T(8,128)(2,1)S(1)} %copy.123.refs_1_, bf16[2,3,32,640]{3,2,1,0:T(8,128)(2,1)S(1)} %copy.124.refs_2_, ...), custom_call_target="tpu_custom_call" | custom-call | flops 6039797760 | bytes 4000000 | tf_op jit(solution)/shard_map/own_part_0/pallas_call | solution.py:294
  33.0 1.1 copy-done.8
  34.1 0.4 collective-permute-done.5
  34.6 4.5 %collective-permute-done.4 = bf16[3,3,32,640]{3,2,0,1:T(8,128)(2,1)S(1)} collective-permute-done((bf16[3,3,32,640]{3,2,0,1:T(8,128)(2,1)S(1)}, bf16[3,3,32,640]{3,2,0,1:T(8,128)(2,1)S(1)}, u32[]{:S(2)}, u32[]{:S(2)}) %collective-permute-start.4) | collective-permute-done | bytes 368672 | tf_op jit(solution)/shard_map/ppermute | solution.py:337
  39.1 5.1 %side_part_0.1 = (bf16[64,512]{1,0:T(8,128)(2,1)S(1)}, f32[64,8,384]{2,1,0:T(8,128)S(1)}, f32[64,8,384]{2,1,0:T(8,128)S(1)}, bf16[2,384,288]{2,1,0:T(8,128)(2,1)S(1)}, s32[2]{0:T(128)S(1)}) custom-call(s32[2]{0:T(128)S(1)} %bitcast.39, bf16[3,3,32,640]{3,2,1,0:T(8,128)(2,1)S(1)} %copy.126.refs_1_, bf16[3,3,32,640]{3,2,1,0:T(8,128)(2,1)S(1)} %copy.127.refs_2_, ...), custom_call_target="tpu_custom_call" | custom-call | flops 3019898880 | bytes 4000000 | tf_op jit(solution)/shard_map/side_part_0/pallas_call | solution.py:323
  44.2 0.7 collective-permute-start.6
  44.9 2.0 %collective-permute-start.7 = (bf16[2,32,512]{2,1,0:T(8,128)(2,1)S(1)}, bf16[2,32,512]{2,1,0:T(8,128)(2,1)S(1)}, u32[]{:S(2)}, u32[]{:S(2)}) collective-permute-start(bf16[2,32,512]{2,1,0:T(8,128)(2,1)S(1)} %bitcast.34), channel_id=1, source_target_pairs={{1,0},{2,1},{3,2},{0,3},{5,4},{6,5},{7,6},{4,7},{9,8},{10,9},{11,1... | collective-permute-start | bytes 196616 | tf_op jit(solution)/shard_map/ppermute | solution.py:337
  47.0 0.1 copy.133.refs_10_
  47.1 1.5 %collective-permute-done.6 = bf16[2,32,512]{2,1,0:T(8,128)(2,1)S(1)} collective-permute-done((bf16[2,32,512]{2,1,0:T(8,128)(2,1)S(1)}, bf16[2,32,512]{2,1,0:T(8,128)(2,1)S(1)}, u32[]{:S(2)}, u32[]{:S(2)}) %collective-permute-start.6) | collective-permute-done | bytes 65568 | tf_op jit(solution)/shard_map/ppermute | solution.py:337
  48.6 4.8 %collective-permute-start.8 = (bf16[2,3,32,512]{3,2,0,1:T(8,128)(2,1)S(1)}, bf16[2,3,32,512]{3,2,0,1:T(8,128)(2,1)S(1)}, u32[]{:S(2)}, u32[]{:S(2)}) collective-permute-start(bf16[2,3,32,512]{3,2,0,1:T(8,128)(2,1)S(1)} %pad_maximum_fusion.5), channel_id=1, source_target_pairs={{12,0},{0,4},{4,8},{8,12},{13,1},{1,5},{5,9},{9,13},{14,2},{2,6},{... | collective-permute-start | bytes 589832 | tf_op jit(solution)/shard_map/ppermute | solution.py:337
  53.5 4.0 %collective-permute-done.8 = bf16[2,3,32,512]{3,2,0,1:T(8,128)(2,1)S(1)} collective-permute-done((bf16[2,3,32,512]{3,2,0,1:T(8,128)(2,1)S(1)}, bf16[2,3,32,512]{3,2,0,1:T(8,128)(2,1)S(1)}, u32[]{:S(2)}, u32[]{:S(2)}) %collective-permute-start.8) | collective-permute-done | bytes 196640 | tf_op jit(solution)/shard_map/ppermute | solution.py:337
  57.5 2.5 %collective-permute-done.9 = bf16[2,3,32,512]{3,2,0,1:T(8,128)(2,1)S(1)} collective-permute-done((bf16[2,3,32,512]{3,2,0,1:T(8,128)(2,1)S(1)}, bf16[2,3,32,512]{3,2,0,1:T(8,128)(2,1)S(1)}, u32[]{:S(2)}, u32[]{:S(2)}) %collective-permute-start.9) | collective-permute-done | bytes 196640 | tf_op jit(solution)/shard_map/ppermute | solution.py:337
  60.1 18.0 %collective-permute-start.11 = (bf16[3,3,32,512]{3,2,0,1:T(8,128)(2,1)S(1)}, bf16[3,3,32,512]{3,2,0,1:T(8,128)(2,1)S(1)}, u32[]{:S(2)}, u32[]{:S(2)}) collective-permute-start(bf16[3,3,32,512]{3,2,0,1:T(8,128)(2,1)S(1)} %pad_maximum_fusion.3), channel_id=1, source_target_pairs={{16,0},{32,16},{48,32},{64,48},{80,64},{96,80},{112,96},{0,112},{1... | collective-permute-start | bytes 884744 | tf_op jit(solution)/shard_map/ppermute | solution.py:337
  78.1 0.1 collective-permute-start.10
  78.3 2.9 %own_part_1.1.refs_4_ = f32[16,8,512]{2,1,0:T(8,128)S(1)} custom-call(s32[2]{0:T(128)S(1)} %bitcast.40, bf16[2,3,32,512]{3,2,1,0:T(8,128)(2,1)S(1)} %copy.128.refs_1_, bf16[2,3,32,512]{3,2,1,0:T(8,128)(2,1)S(1)} %copy.129.refs_2_, bf16[2,3,32,512]{3,2,1,0:T(8,128)(2,1)S(1)} %copy.130.refs_3_, bf16[2,64,16]{2,1,0:T(8,128)(2,1)S(1)} %multiply_bitcast_fusion.refs_4_.refs_5_, ...), custom_call_target="tpu_custom_call" | custom-call | flops 6039797760 | bytes 4000000 | tf_op jit(solution)/shard_map/own_part_1/pallas_call | solution.py:294
  81.2 3.3 %collective-permute-done.11 = bf16[3,3,32,512]{3,2,0,1:T(8,128)(2,1)S(1)} collective-permute-done((bf16[3,3,32,512]{3,2,0,1:T(8,128)(2,1)S(1)}, bf16[3,3,32,512]{3,2,0,1:T(8,128)(2,1)S(1)}, u32[]{:S(2)}, u32[]{:S(2)}) %collective-permute-start.11) | collective-permute-done | bytes 294944 | tf_op jit(solution)/shard_map/ppermute | solution.py:337
  84.5 4.5 %collective-permute-done.10 = bf16[3,3,32,512]{3,2,0,1:T(8,128)(2,1)S(1)} collective-permute-done((bf16[3,3,32,512]{3,2,0,1:T(8,128)(2,1)S(1)}, bf16[3,3,32,512]{3,2,0,1:T(8,128)(2,1)S(1)}, u32[]{:S(2)}, u32[]{:S(2)}) %collective-permute-start.10) | collective-permute-done | bytes 294944 | tf_op jit(solution)/shard_map/ppermute | solution.py:337
  89.0 3.6 %side_part_1.1 = (bf16[64,512]{1,0:T(8,128)(2,1)S(1)}, f32[128,128]{1,0:T(8,128)}) custom-call(s32[2]{0:T(128)S(1)} %bitcast.41, bf16[3,3,32,512]{3,2,1,0:T(8,128)(2,1)S(1)} %copy.131.refs_1_, bf16[3,3,32,512]{3,2,1,0:T(8,128)(2,1)S(1)} %copy.132.refs_2_, bf16[2,32,512]{2,1,0:T(8,128)(2,1)S(1)} %bitcast.36, f32[16,8,512]{2,1,0:T(8,128)S(1)} %own_part_1.1.refs_4_, ...), custom_call_target="tpu_custom_call" | custom-call | flops 3019898880 | bytes 4000000 | tf_op jit(solution)/shard_map/side_part_1/pallas_call | solution.py:323
  92.6 15.5 %all-to-all-start = ((f32[128,1,128]{2,1,0:T(1,128)}), f32[128,1,128]{2,1,0:T(1,128)S(1)}, u32[]{:S(2)}, u32[]{:S(2)}) async-start(f32[128,1,128]{2,1,0:T(1,128)} %bitcast.19), calls=%async_computation | async-start | bytes 131072 | tf_op jit(solution)/shard_map/all_to_all | solution.py:412
  108.1 0.6 slice.69
  108.7 0.6 copy.136
  109.3 8.4 %all-to-all-done = f32[128,1,128]{2,1,0:T(1,128)S(1)} async-done(((f32[128,1,128]{2,1,0:T(1,128)}), f32[128,1,128]{2,1,0:T(1,128)S(1)}, u32[]{:S(2)}, u32[]{:S(2)}) %all-to-all-start) | async-done | bytes 65568 | tf_op jit(solution)/shard_map/all_to_all | solution.py:412
  117.8 0.7 reduce_sum.9
  (67 shorter events, 0.7 us)
Async XLA Ops:
  4.0 7.2 %collective-permute-start = (bf16[2,32,640]{2,1,0:T(8,128)(2,1)S(1)}, bf16[2,32,640]{2,1,0:T(8,128)(2,1)S(1)}, u32[]{:S(2)}, u32[]{:S(2)}) collective-permute-start(bf16[2,32,640]{2,1,0:T(8,128)(2,1)S(1)} %get-tuple-element.62.refs_3_), channel_id=1, source_target_pairs={{3,0},{0,1},{1,2},{2,3},{7,4},{4,5},{5,6},{6,7},{11,8},{8,9},{9,10... | collective-permute-start | bytes 245768 | tf_op jit(solution)/shard_map/ppermute | solution.py:337
  6.1 5.1 %collective-permute-start.1 = (bf16[2,32,640]{2,1,0:T(8,128)(2,1)S(1)}, bf16[2,32,640]{2,1,0:T(8,128)(2,1)S(1)}, u32[]{:S(2)}, u32[]{:S(2)}) collective-permute-start(bf16[2,32,640]{2,1,0:T(8,128)(2,1)S(1)} %get-tuple-element.62.refs_3_), channel_id=1, source_target_pairs={{1,0},{2,1},{3,2},{0,3},{5,4},{6,5},{7,6},{4,7},{9,8},{10,9},{11,1... | collective-permute-start | bytes 245768 | tf_op jit(solution)/shard_map/ppermute | solution.py:337
  11.2 10.6 %collective-permute-start.2 = (bf16[2,3,32,640]{3,2,0,1:T(8,128)(2,1)S(1)}, bf16[2,3,32,640]{3,2,0,1:T(8,128)(2,1)S(1)}, u32[]{:S(2)}, u32[]{:S(2)}) collective-permute-start(bf16[2,3,32,640]{3,2,0,1:T(8,128)(2,1)S(1)} %pad_maximum_fusion.4), channel_id=1, source_target_pairs={{12,0},{0,4},{4,8},{8,12},{13,1},{1,5},{5,9},{9,13},{14,2},{2,6},{... | collective-permute-start | bytes 737288 | tf_op jit(solution)/shard_map/ppermute | solution.py:337
  16.1 7.1 %collective-permute-start.3 = (bf16[2,3,32,640]{3,2,0,1:T(8,128)(2,1)S(1)}, bf16[2,3,32,640]{3,2,0,1:T(8,128)(2,1)S(1)}, u32[]{:S(2)}, u32[]{:S(2)}) collective-permute-start(bf16[2,3,32,640]{3,2,0,1:T(8,128)(2,1)S(1)} %pad_maximum_fusion.4), channel_id=1, source_target_pairs={{4,0},{8,4},{12,8},{0,12},{5,1},{9,5},{13,9},{1,13},{6,2},{10,6},{... | collective-permute-start | bytes 737288 | tf_op jit(solution)/shard_map/ppermute | solution.py:337
  23.3 3.6 %copy-start = (s32[2,1,1]{0,2,1:T(1,128)S(1)}, s32[2,1,1]{0,2,1:T(1,128)}, u32[]{:S(2)}) copy-start(s32[2,1,1]{0,2,1:T(1,128)} %param.13) | copy-start | bytes 28
  23.3 3.6 %copy-start.1 = (bf16[2,128,512]{2,1,0:T(8,128)(2,1)S(1)}, bf16[2,128,512]{2,1,0:T(8,128)(2,1)}, u32[]{:S(2)}) copy-start(bf16[2,128,512]{2,1,0:T(8,128)(2,1)} %refs_9_.3) | copy-start | bytes 786436
  23.3 3.6 %copy-start.2 = (bf16[2,64,512]{2,1,0:T(8,128)(2,1)S(1)}, bf16[2,64,512]{2,1,0:T(8,128)(2,1)}, u32[]{:S(2)}) copy-start(bf16[2,64,512]{2,1,0:T(8,128)(2,1)} %refs_6_.7) | copy-start | bytes 393220
  23.3 3.6 %copy-start.3 = (bf16[2,128,128]{2,1,0:T(8,128)(2,1)S(1)}, bf16[2,128,128]{2,1,0:T(8,128)(2,1)}, u32[]{:S(2)}) copy-start(bf16[2,128,128]{2,1,0:T(8,128)(2,1)} %refs_7_.7) | copy-start | bytes 196612
  23.3 3.6 %copy-start.4 = (f32[2,128]{1,0:T(2,128)S(1)}, f32[2,128]{1,0:T(2,128)}, u32[]{:S(2)}) copy-start(f32[2,128]{1,0:T(2,128)} %refs_8_.7) | copy-start | bytes 3076
  23.4 11.2 %collective-permute-start.5 = (bf16[3,3,32,640]{3,2,0,1:T(8,128)(2,1)S(1)}, bf16[3,3,32,640]{3,2,0,1:T(8,128)(2,1)S(1)}, u32[]{:S(2)}, u32[]{:S(2)}) collective-permute-start(bf16[3,3,32,640]{3,2,0,1:T(8,128)(2,1)S(1)} %pad_maximum_fusion.1), channel_id=1, source_target_pairs={{16,0},{32,16},{48,32},{64,48},{80,64},{96,80},{112,96},{0,112},{1... | collective-permute-start | bytes 1105928 | tf_op jit(solution)/shard_map/ppermute | solution.py:337
  26.7 12.3 %collective-permute-start.4 = (bf16[3,3,32,640]{3,2,0,1:T(8,128)(2,1)S(1)}, bf16[3,3,32,640]{3,2,0,1:T(8,128)(2,1)S(1)}, u32[]{:S(2)}, u32[]{:S(2)}) collective-permute-start(bf16[3,3,32,640]{3,2,0,1:T(8,128)(2,1)S(1)} %pad_maximum_fusion), channel_id=1, source_target_pairs={{112,0},{0,16},{16,32},{32,48},{48,64},{64,80},{80,96},{96,112},{1... | collective-permute-start | bytes 1105928 | tf_op jit(solution)/shard_map/ppermute | solution.py:337
  33.0 1.1 copy-start.8
  34.1 10.0 %copy-start.6 = (f32[64,8,640]{2,1,0:T(8,128)}, f32[64,8,640]{2,1,0:T(8,128)S(1)}, u32[]{:S(2)}) copy-start(f32[64,8,640]{2,1,0:T(8,128)S(1)} %get-tuple-element.17.refs_9_) | copy-start | bytes 3932164
  34.1 10.1 %copy-start.10 = (bf16[640,576]{1,0:T(8,128)(2,1)}, bf16[640,576]{1,0:T(8,128)(2,1)S(1)}, u32[]{:S(2)}) copy-start(bf16[640,576]{1,0:T(8,128)(2,1)S(1)} %get-tuple-element.19.refs_11_) | copy-start | bytes 2211844
  39.1 7.9 %copy-start.12 = (bf16[128,64]{0,1:T(8,128)(2,1)S(1)}, bf16[128,64]{0,1:T(8,128)(2,1)}, u32[]{:S(2)}) copy-start(bf16[128,64]{0,1:T(8,128)(2,1)} %param.22) | copy-start | bytes 49156
  44.2 4.4 %collective-permute-start.6 = (bf16[2,32,512]{2,1,0:T(8,128)(2,1)S(1)}, bf16[2,32,512]{2,1,0:T(8,128)(2,1)S(1)}, u32[]{:S(2)}, u32[]{:S(2)}) collective-permute-start(bf16[2,32,512]{2,1,0:T(8,128)(2,1)S(1)} %bitcast.33), channel_id=1, source_target_pairs={{3,0},{0,1},{1,2},{2,3},{7,4},{4,5},{5,6},{6,7},{11,8},{8,9},{9,10... | collective-permute-start | bytes 196616 | tf_op jit(solution)/shard_map/ppermute | solution.py:337
  44.9 3.7 %collective-permute-start.7 = (bf16[2,32,512]{2,1,0:T(8,128)(2,1)S(1)}, bf16[2,32,512]{2,1,0:T(8,128)(2,1)S(1)}, u32[]{:S(2)}, u32[]{:S(2)}) collective-permute-start(bf16[2,32,512]{2,1,0:T(8,128)(2,1)S(1)} %bitcast.34), channel_id=1, source_target_pairs={{1,0},{2,1},{3,2},{0,3},{5,4},{6,5},{7,6},{4,7},{9,8},{10,9},{11,1... | collective-permute-start | bytes 196616 | tf_op jit(solution)/shard_map/ppermute | solution.py:337
  48.6 8.9 %collective-permute-start.8 = (bf16[2,3,32,512]{3,2,0,1:T(8,128)(2,1)S(1)}, bf16[2,3,32,512]{3,2,0,1:T(8,128)(2,1)S(1)}, u32[]{:S(2)}, u32[]{:S(2)}) collective-permute-start(bf16[2,3,32,512]{3,2,0,1:T(8,128)(2,1)S(1)} %pad_maximum_fusion.5), channel_id=1, source_target_pairs={{12,0},{0,4},{4,8},{8,12},{13,1},{1,5},{5,9},{9,13},{14,2},{2,6},{... | collective-permute-start | bytes 589832 | tf_op jit(solution)/shard_map/ppermute | solution.py:337
  53.4 6.6 %collective-permute-start.9 = (bf16[2,3,32,512]{3,2,0,1:T(8,128)(2,1)S(1)}, bf16[2,3,32,512]{3,2,0,1:T(8,128)(2,1)S(1)}, u32[]{:S(2)}, u32[]{:S(2)}) collective-permute-start(bf16[2,3,32,512]{3,2,0,1:T(8,128)(2,1)S(1)} %pad_maximum_fusion.5), channel_id=1, source_target_pairs={{4,0},{8,4},{12,8},{0,12},{5,1},{9,5},{13,9},{1,13},{6,2},{10,6},{... | collective-permute-start | bytes 589832 | tf_op jit(solution)/shard_map/ppermute | solution.py:337
  53.4 24.8 %copy-start.11 = (bf16[640,576]{1,0:T(8,128)(2,1)S(1)}, bf16[640,576]{1,0:T(8,128)(2,1)}, u32[]{:S(2)}) copy-start(bf16[640,576]{1,0:T(8,128)(2,1)} %copy-done.10) | copy-start | bytes 2211844
  53.5 24.8 %copy-start.7 = (f32[64,8,640]{2,1,0:T(8,128)S(1)}, f32[64,8,640]{2,1,0:T(8,128)}, u32[]{:S(2)}) copy-start(f32[64,8,640]{2,1,0:T(8,128)} %copy-done.6) | copy-start | bytes 3932164
  53.5 24.8 %copy-start.9 = (f32[64,8,640]{2,1,0:T(8,128)S(1)}, f32[64,8,640]{2,1,0:T(8,128)}, u32[]{:S(2)}) copy-start(f32[64,8,640]{2,1,0:T(8,128)} %copy-done.8) | copy-start | bytes 3932164
  60.1 24.4 %collective-permute-start.11 = (bf16[3,3,32,512]{3,2,0,1:T(8,128)(2,1)S(1)}, bf16[3,3,32,512]{3,2,0,1:T(8,128)(2,1)S(1)}, u32[]{:S(2)}, u32[]{:S(2)}) collective-permute-start(bf16[3,3,32,512]{3,2,0,1:T(8,128)(2,1)S(1)} %pad_maximum_fusion.3), channel_id=1, source_target_pairs={{16,0},{32,16},{48,32},{64,48},{80,64},{96,80},{112,96},{0,112},{1... | collective-permute-start | bytes 884744 | tf_op jit(solution)/shard_map/ppermute | solution.py:337
  78.1 10.8 %collective-permute-start.10 = (bf16[3,3,32,512]{3,2,0,1:T(8,128)(2,1)S(1)}, bf16[3,3,32,512]{3,2,0,1:T(8,128)(2,1)S(1)}, u32[]{:S(2)}, u32[]{:S(2)}) collective-permute-start(bf16[3,3,32,512]{3,2,0,1:T(8,128)(2,1)S(1)} %pad_maximum_fusion.2), channel_id=1, source_target_pairs={{112,0},{0,16},{16,32},{32,48},{48,64},{64,80},{80,96},{96,112},{1... | collective-permute-start | bytes 884744 | tf_op jit(solution)/shard_map/ppermute | solution.py:337
  78.3 10.7 %copy-start.5 = (f32[64]{0:T(128)S(1)}, f32[64]{0:T(128)}, u32[]{:S(2)}) copy-start(f32[64]{0:T(128)} %param.23) | copy-start | bytes 772
  92.6 25.2 %all-to-all-start = ((f32[128,1,128]{2,1,0:T(1,128)}), f32[128,1,128]{2,1,0:T(1,128)S(1)}, u32[]{:S(2)}, u32[]{:S(2)}) async-start(f32[128,1,128]{2,1,0:T(1,128)} %bitcast.19), calls=%async_computation | async-start | bytes 131072 | tf_op jit(solution)/shard_map/all_to_all | solution.py:412

commit v3 on v2

--- a/solution.py
+++ b/solution.py
@@ -3,6 +3,7 @@
 
 import jax
 import jax.numpy as jnp
+import numpy as np
 from jax import lax
 from jax.experimental import pallas as pl
 from jax.experimental.pallas import tpu as pltpu
@@ -13,8 +14,9 @@
 slots = 32
 chan = 128
 hidden = 64
-block = 4
-blocks = slots // block
+block = 8
+room = 2 * slots + block
+depth = 80
 own_atoms, own_main, own_span = 576, 512, 640
 side_atoms, side_main, side_span = 288, 256, 384
 f32 = jnp.float32
@@ -68,28 +70,27 @@
     return flag(row == rank).astype(bf16)
 
 
-def geometry(q, row, mine, shift, basis_ref, wts_ref, at):
+def geometry(row, mine, number, shift, basis_ref, wts_ref, at):
     dist2 = None
     disp = []
     for k in range(3):
-        other = row[k : k + 1] + (row[4 + k : 5 + k] + (shift if k == 0 else 0.0))
-        d = other - mine[:, k : k + 1]
+        offset = row[4 + k : 5 + k] + shift if k == 0 else row[4 + k : 5 + k]
+        d = (row[k : k + 1] + offset) - mine[:, k : k + 1]
         disp.append(d)
         dist2 = d * d if k == 0 else dist2 + d * d
     live = row[3:4]
-    number = lax.broadcasted_iota(jnp.int32, dist2.shape, 0) + (q * slots + 1)
     itself = flag(row[7:8] == number.astype(f32))
     dist = jnp.sqrt(dist2 + itself + (1.0 - live))
     smooth = jnp.where(dist < cutoff, 0.5 * (jnp.cos(math.pi * dist / cutoff) + 1.0), 0.0)
     weight = smooth * live * (1.0 - itself)
     scaled = weight / dist
-    wts_ref[at, 0, :] = weight
+    wts_ref[0, at, :] = weight
     for k in range(3):
-        wts_ref[at, 1 + k, :] = scaled * disp[k]
+        wts_ref[1 + k, at, :] = scaled * disp[k]
     sharp = 0.5 * (7.0 / cutoff) ** 2
     for k in range(8):
         away = dist - k * (cutoff / 7.0)
-        basis_ref[at, k, :] = jnp.exp(-sharp * (away * away))
+        basis_ref[k, at, :] = jnp.exp(-sharp * (away * away))
 
 
 def features(layer, x, part, weights, feats):
@@ -106,40 +107,73 @@
         feats[1 + k][part, :] = jnp.concatenate([gc, gg * vec[k]], axis=1)
 
 
-def messages(layer, q, count, window, weights, basis_ref, wts_ref, feats, edges, delta):
+def messages(layer, base, count, window, weights, basis_ref, wts_ref, feats, edges, delta):
     rin_ref, rout_ref = weights[:2]
     width = window.stop - window.start
-
-    def one_block(b, carry):
-        for r in range(block):
-            i = q * slots + b * block + r
-            wide = jnp.concatenate(
-                [basis_ref[i][:, window], jnp.ones((8, width), f32)], axis=0
-            ).astype(bf16)
-            s = half_silu(dot(rin_ref[layer], wide)).astype(bf16).reshape(4, 16, width)
-            part = slice(r * hidden, (r + 1) * hidden)
-            w = wts_ref[i][:, window]
-            for g in range(4):
-                line = jnp.broadcast_to(w[g : g + 1, :], (16, width)).astype(bf16)
-                edges[g][part, :width] = (s * line[None]).reshape(hidden, width)
-        plain = dot(edges[0][:, :width], feats[0][window, :])
-        turned = [dot(edges[k + 1][:, :width], feats[k + 1][window, :]) for k in range(3)]
+    even, odd = edges[:4], edges[4:]
+
+    def rows_at(b):
+        return pl.ds(pl.multiple_of(base + b * block, block), block)
+
+    def hidden_of(b):
+        slab = basis_ref[:, rows_at(b), window].reshape(8 * block, width)
+        slab = jnp.concatenate([slab, jnp.ones((depth - 8 * block, width), f32)], axis=0)
+        return dot(rin_ref[layer], slab.astype(bf16)), wts_ref[:, rows_at(b), window]
+
+    def edge(r, y, w, out):
+        part = slice(r * hidden, (r + 1) * hidden)
+        s = half_silu(y[part]).astype(bf16).reshape(4, 16, width)
+        for g in range(4):
+            line = jnp.broadcast_to(w[g][r : r + 1, :], (16, width)).astype(bf16)
+            out[g][part, :width] = (s * line[None]).reshape(hidden, width)
+
+    def product(n, used):
+        if n < 2:
+            return dot(used[0][:, :width], feats[0][window, 2 * n * chan : 2 * (n + 1) * chan])
+        return dot(used[n - 1][:, :width], feats[n - 1][window, :])
+
+    def gather(n, result, radial, sums):
+        groups = ((0, 1), (1, 1), (2, 3), (2, 3), (2, 3))[n]
+        targets = ((0, 1), (2, 3), (1, 0), (2, 0), (3, 0))[n]
+        for half in range(2):
+            value = result[:, half * chan : (half + 1) * chan].reshape(block, hidden, chan)
+            value = jnp.sum(value * radial[groups[half]], axis=1)
+            t = targets[half]
+            sums[t] = value if sums[t] is None else sums[t] + value
+
+    def step(b, used, following):
         radial = [rout_ref[layer, :, g * chan : (g + 1) * chan].astype(f32)[None] for g in range(4)]
-        split = (block, hidden, chan)
-        proj = turned[0][:, chan:] + turned[1][:, chan:] + turned[2][:, chan:]
-        totals = [plain[:, :chan].reshape(split) * radial[0] + proj.reshape(split) * radial[3]]
-        for k in range(3):
-            totals.append(
-                plain[:, (k + 1) * chan : (k + 2) * chan].reshape(split) * radial[1]
-                + turned[k][:, :chan].reshape(split) * radial[2]
-            )
-        at = q * blocks + b
+        sums = [None] * 4
+        if following is not None:
+            y, w = hidden_of(b + 1)
+        made, previous = 0, None
+        for n in range(5):
+            result = product(n, used)
+            while following is not None and made < block and made * 5 < (n + 1) * block:
+                edge(made, y, w, following)
+                made += 1
+            if n > 0:
+                gather(n - 1, previous, radial, sums)
+            previous = result
+        gather(4, previous, radial, sums)
         for g in range(4):
-            lanes = slice(g * chan, (g + 1) * chan)
-            delta[at, 0:block, lanes] += jnp.sum(totals[g], axis=1)
+            delta[rows_at(b), g * chan : (g + 1) * chan] += sums[g]
+
+    count = (count + block - 1) // block
+    y, w = hidden_of(0)
+    for r in range(block):
+        edge(r, y, w, even)
+
+    def two_steps(t, carry):
+        step(2 * t, even, odd)
+        step(2 * t + 1, odd, even)
         return carry
 
-    lax.fori_loop(0, (count + block - 1) // block, one_block, 0)
+    lax.fori_loop(0, count // 2, two_steps, 0)
+
+    @pl.when(count % 2 == 1)
+    def _():
+        step(count - 1, even, None)
 
 
 def own_kernel(layer, *refs):
@@ -152,7 +186,7 @@
     else:
         basis, wts, order, more, delta = refs[:5]
         refs = refs[5:]
-    feats, edges = refs[:4], refs[4:8]
+    feats, edges = refs[:4], refs[4:12]
     parts = [ref[...].reshape(own_atoms // 3, -1) for ref in (low, middle, high)]
     third = own_atoms // 3
     if layer == 0:
@@ -162,10 +196,16 @@
         row = rows_of(dot(order[...], geo).astype(bf16))
         total = jnp.sum(live)
         more[0] = jnp.where(total > own_main + 0.5, 1, 0)
-        for q in range(2):
-            mine = columns_of(middle[q, 1][:, 4 * chan :])
-            at = slice(q * slots, (q + 1) * slots)
-            geometry(q, row, mine, -q * cutoff, basis, wts, at)
+        first = counts_ref[0]
+        mine = columns_of(
+            jnp.concatenate([middle[q, 1][:, 4 * chan :] for q in range(2)], axis=0)
+        )
+        place = lax.broadcasted_iota(jnp.int32, (2 * slots, 1), 0)
+        moved = pltpu.roll(mine, lax.rem(first + slots, 2 * slots), 0)
+        mine = jnp.where(place < first, mine, moved)
+        number = jnp.where(place < first, place + 1, place - first + (slots + 1))
+        shift = jnp.where(place < first, 0.0, -cutoff)
+        geometry(row, mine, number, shift, basis, wts, slice(0, 2 * slots))
 
     def gathered(part):
         x = None
@@ -176,15 +216,14 @@
 
     delta[...] = jnp.zeros_like(delta)
     main, rest = slice(0, own_main), slice(own_main, own_span)
+    count = counts_ref[0] + counts_ref[1]
     gathered(main)
-    for q in range(2):
-        messages(layer, q, counts_ref[q], main, weights, basis, wts, feats, edges, delta)
+    messages(layer, 0, count, main, weights, basis, wts, feats, edges, delta)
 
     @pl.when(more[0] > 0)
     def _():
         gathered(rest)
-        for q in range(2):
-            messages(layer, q, counts_ref[q], rest, weights, basis, wts, feats, edges, delta)
+        messages(layer, 0, count, rest, weights, basis, wts, feats, edges, delta)
 
 
 def side_kernel(layer, last, *refs):
@@ -203,8 +242,8 @@
         energy_ref, refs = refs[0], refs[1:]
     if layer == 0:
         (basis, wts, order, more), refs = refs[:4], refs[4:]
-    feats, edges, delta = refs[:4], refs[4:8], refs[8]
-    delta[...] = before[...]
+    feats, edges, delta = refs[:4], refs[4:12], refs[12]
+    delta[...] = jnp.zeros_like(delta)
     main, rest = slice(0, side_main), slice(side_main, side_span)
     for q in range(2):
         x_all = (low, high)[q][...].reshape(side_atoms, -1)
@@ -217,25 +256,28 @@
             more[q] = jnp.where(total > side_main + 0.5, 1, 0)
             mine = columns_of(own_ref[q][:, 4 * chan :])
             at = slice(q * slots, (q + 1) * slots)
-            geometry(q, row, mine, (-cutoff, cutoff)[q], basis, wts, at)
+            number = lax.broadcasted_iota(jnp.int32, (slots, 1), 0) + (q * slots + 1)
+            geometry(row, mine, number, (-cutoff, cutoff)[q], basis, wts, at)
 
         def gathered(part, q=q, x_all=x_all):
             x = dot(order[q, part, :], x_all[:, : 4 * chan])
             features(layer, x.astype(bf16), part, weights, feats)
 
         gathered(main)
-        messages(layer, q, counts_ref[q], main, weights, basis, wts, feats, edges, delta)
+        messages(layer, q * slots, counts_ref[q], main, weights, basis, wts, feats, edges, delta)
 
         @pl.when(more[q] > 0)
         def _(q=q, gathered=gathered):
             gathered(rest)
-            messages(layer, q, counts_ref[q], rest, weights, basis, wts, feats, edges, delta)
+            messages(layer, q * slots, counts_ref[q], rest, weights, basis, wts, feats, edges, delta)
 
     slot = lax.broadcasted_iota(jnp.int32, (2 * slots, 1), 0)
     limit = jnp.where(slot < slots, counts_ref[0], counts_ref[1] + slots)
     live = flag(slot < limit)
     mine = own_ref[...].reshape(2 * slots, -1)[:, : 4 * chan].astype(f32)
-    change = jnp.concatenate([delta[b, 0:block, :] for b in range(2 * blocks)], axis=0)
+    packed = before[0 : 2 * slots, :]
+    moved = pltpu.roll(packed, slots - counts_ref[0], 0)
+    change = delta[0 : 2 * slots, :] + jnp.where(slot < slots, packed, moved)
     state = ((mine + message_scale * change) * live).astype(bf16)
     state_ref[...] = state
     if last:
@@ -252,7 +294,7 @@
     return [
         pltpu.VMEM((span, 4 * chan), bf16),
         *[pltpu.VMEM((span, 2 * chan), bf16)] * 3,
-        *[pltpu.VMEM((block * hidden, main), bf16)] * 4,
+        *[pltpu.VMEM((block * hidden, main), bf16)] * 8,
     ]
 
 
@@ -263,14 +305,13 @@
 
 
 params = pltpu.CompilerParams(vmem_limit_bytes=40 * 1024 * 1024)
-delta_shape = jax.ShapeDtypeStruct((2 * blocks, 8, 4 * chan), f32)
+delta_shape = jax.ShapeDtypeStruct((room, 4 * chan), f32)
 
 
 def kept_shapes(span, order):
-    pairs = jax.ShapeDtypeStruct((2 * slots, 8, span), f32)
     return (
-        pairs,
-        pairs,
+        jax.ShapeDtypeStruct((8, room, span), f32),
+        jax.ShapeDtypeStruct((4, room, span), f32),
         jax.ShapeDtypeStruct(order, bf16),
         jax.ShapeDtypeStruct((2,), jnp.int32),
     )
@@ -338,17 +379,28 @@
 
 
 def tables():
-    j = lax.broadcasted_iota(jnp.int32, (own_atoms, chan), 0)
-    lane = lax.broadcasted_iota(jnp.int32, (own_atoms, chan), 1)
+    j = np.arange(own_atoms)
     slot, z, plane, y = j % slots, j // slots % 3, j // (3 * slots) % 2, j // (6 * slots)
-    name = jnp.where((y == 1) & (z == 1), plane * slots + slot + 1, 0)
-    values = jnp.where(lane == 4, plane * 5, 0) + jnp.where(lane == 7, name, 0)
-    values += jnp.where(lane == 5, (y - 1) * 5, 0) + jnp.where(lane == 6, (z - 1) * 5, 0)
-    own = values.astype(bf16)
-    j, lane = j[:side_atoms], lane[:side_atoms]
-    z, y = j // slots % 3, j // (3 * slots)
-    values = jnp.where(lane == 5, (y - 1) * 5, 0) + jnp.where(lane == 6, (z - 1) * 5, 0)
-    return own, values.astype(bf16)
+    own = np.zeros((own_atoms, chan), np.float32)
+    own[:, 4], own[:, 5], own[:, 6] = plane * 5, (y - 1) * 5, (z - 1) * 5
+    own[:, 7] = np.where((y == 1) & (z == 1), plane * slots + slot + 1, 0)
+    j = np.arange(side_atoms)
+    side = np.zeros((side_atoms, chan), np.float32)
+    side[:, 5], side[:, 6] = (j // (3 * slots) - 1) * 5, (j // slots % 3 - 1) * 5
+    return jnp.asarray(own, bf16), jnp.asarray(side, bf16)
+
+
+def radial_rows(radial_in, radial_bias):
+    layers = radial_in.shape[0]
+    eye = jnp.asarray(np.eye(block) * 0.5, bf16)
+    spread = radial_in.transpose(0, 2, 1)[:, None, :, :, None] * eye[:, None, None, :]
+    spread = spread.reshape(layers, block * hidden, 8 * block)
+    bias = jnp.stack([p * jnp.asarray(0.5, bf16) for p in pieces(radial_bias)], axis=2)
+    bias = jnp.broadcast_to(bias[:, None], (layers, block, hidden, 3))
+    bias = bias.reshape(layers, block * hidden, 3)
+    return jnp.pad(
+        jnp.concatenate([spread, bias], axis=2), ((0, 0), (0, 0), (0, depth - 8 * block - 3))
+    )
 
 
 def on_device(
@@ -380,19 +432,15 @@
         axis=2,
     )
     layers = radial_in.shape[0]
-    rin = jnp.concatenate(
-        [radial_in]
-        + [p[:, None, :] for p in pieces(radial_bias)]
-        + [jnp.zeros((layers, 5, hidden), bf16)],
-        axis=1,
-    )
-    rin = (rin * jnp.asarray(0.5, bf16)).transpose(0, 2, 1)
-    weights = [rin, radial_out, atom_in, atom_bias, atom_out]
     own_table, side_table = tables()
     own_kept = side_kept = ()
     for layer in range(layers):
         last = layer == layers - 1
         y = jnp.stack([shifted(own, "gz", -1), own, shifted(own, "gz", 1)], axis=1)
+        if layer == 0:
+            y, radial_in, radial_bias = lax.optimization_barrier((y, radial_in, radial_bias))
+            rin = radial_rows(radial_in, radial_bias)
+            weights = [rin, radial_out, atom_in, atom_bias, atom_out]
         ys = [shifted(y, "gy", -1), y, shifted(y, "gy", 1)]
         low = shifted(jnp.stack([v[1] for v in ys]), "gx", -1)
         high = shifted(jnp.stack([v[0] for v in ys]), "gx", 1)

time: 120 us -> 106 us (0.88)
  starting transfers between devices: 52.9 us -> 38.8 us
  Pallas kernels: 17.6 us -> 20.6 us
  other arithmetic: 4.88 us -> 2.78 us
  waiting for transfers between devices: 36.1 us -> 34.9 us
    ppermute x12, starting transfers between devices: 37.4 us -> 25.7 us  [shifted(): lax.ppermute(value, axis, [((i + step) % count, i) for i in range(count)])]
    all_to_all x1, starting transfers between devices: 15.5 us -> 13.1 us  [on_device(): every = lax.all_to_all(energy, ('gx', 'gy', 'gz'), 0, 0, tiled=True)]
    convert_element_type x2 -> x0, other arithmetic: 1.56 us -> none  [the longest x1 1.26 us: tables(): own = values.astype(bf16)]
    pallas_call x2, Pallas kernels: 8.97 us -> 10.5 us  [own_call(): pl.pallas_call(functools.partial(own_kernel, layer), out_shape=shapes, in...]
    pallas_call x2, Pallas kernels: 8.68 us -> 10.1 us  [side_call(): pl.pallas_call(functools.partial(side_kernel, layer, last), out_shape=sha...]
    mul x0 -> x6, local copies, waits for them, and re-layouts: none -> 1.44 us  [radial_rows(): radial_in.transpose(0, 2, 1)[:, None, :, :, None] * eye[:, None, None, :]]
    ppermute x12, waiting for transfers between devices: 27.7 us -> 26.4 us  [shifted(): lax.ppermute(value, axis, [((i + step) % count, i) for i in range(count)])]
    unnamed x31 -> x38, local copies, waits for them, and re-layouts: 4.24 us -> 3.2 us
  transfers between devices with their start and end apart: 13 -> 13, of which waited for: 10 -> 12; matrix products, arithmetic and copies ran while one was open for 5% -> 3% of each run, Pallas kernels for 8% -> 10%
where the time goes in v3:
time: 106 us; the launch traced here: 104 us
  starting transfers between devices  38.8 us (37%)
  waiting for transfers between devices  34.9 us (33%)
  Pallas kernels  20.6 us (19%)
  local copies, waits for them, and re-layouts  5.92 us (6%)
  other arithmetic  2.78 us (3%)
  between operations  1.12 us (1%)
    ppermute x12, waiting for transfers between devices, shifted(): lax.ppermute(value, axis, [((i + step) % count, i) for i in range(count)])  26.4 us
    ppermute x12, starting transfers between devices, shifted(): lax.ppermute(value, axis, [((i + step) % count, i) for i in range(count)])  25.7 us
    all_to_all x1, starting transfers between devices, on_device(): every = lax.all_to_all(energy, ('gx', 'gy', 'gz'), 0, 0, tiled=True)  13.1 us
    pallas_call x2, Pallas kernels, own_call(): pl.pallas_call(functools.partial(own_kernel, layer), out_shape=shapes, in...  10.5 us
    pallas_call x2, Pallas kernels, side_call(): pl.pallas_call(functools.partial(side_kernel, layer, last), out_shape=sha...  10.1 us
    all_to_all x1, waiting for transfers between devices, on_device(): every = lax.all_to_all(energy, ('gx', 'gy', 'gz'), 0, 0, tiled=True)  8.42 us
    unnamed x38, local copies, waits for them, and re-layouts  3.2 us
  transfers between devices with their start and end apart: 13, of which 12 were waited for; matrix products, arithmetic and copies ran while one was open for 3% of the time, Pallas kernels for 10%

profile of v3, /device:TPU:1, one launch (start us, length us, event | category | flops | bytes accessed | tf_op | source)
XLA Modules:
  0.0 104.1 jit_solution(12980901336887546866)
XLA Ops:
  0.7 0.7 fusion.8
  1.4 0.7 copy.134
  2.1 0.1 copy.115
  2.2 0.1 maximum_bitcast_fusion
  2.3 0.8 copy.113
  3.2 0.1 fusion.10
  3.3 0.7 fusion.15
  4.0 2.1 %collective-permute-start = (bf16[2,32,640]{2,1,0:T(8,128)(2,1)S(1)}, bf16[2,32,640]{2,1,0:T(8,128)(2,1)S(1)}, u32[]{:S(2)}, u32[]{:S(2)}) collective-permute-start(bf16[2,32,640]{2,1,0:T(8,128)(2,1)S(1)} %get-tuple-element.64.refs_3_), channel_id=1, source_target_pairs={{3,0},{0,1},{1,2},{2,3},{7,4},{4,5},{5,6},{6,7},{11,8},{8,9},{9,10... | collective-permute-start | bytes 245768 | tf_op jit(solution)/shard_map/ppermute | solution.py:378
  6.1 1.3 %collective-permute-start.1 = (bf16[2,32,640]{2,1,0:T(8,128)(2,1)S(1)}, bf16[2,32,640]{2,1,0:T(8,128)(2,1)S(1)}, u32[]{:S(2)}, u32[]{:S(2)}) collective-permute-start(bf16[2,32,640]{2,1,0:T(8,128)(2,1)S(1)} %get-tuple-element.64.refs_3_), channel_id=1, source_target_pairs={{1,0},{2,1},{3,2},{0,3},{5,4},{6,5},{7,6},{4,7},{9,8},{10,9},{11,1... | collective-permute-start | bytes 245768 | tf_op jit(solution)/shard_map/ppermute | solution.py:378
  7.5 0.8 mul.31
  8.2 0.1 mul.32
  8.4 0.1 copy.116
  8.5 0.7 collective-permute-done
  9.2 0.2 collective-permute-done.1
  9.4 5.7 %collective-permute-start.2 = (bf16[2,3,32,640]{3,2,0,1:T(8,128)(2,1)S(1)}, bf16[2,3,32,640]{3,2,0,1:T(8,128)(2,1)S(1)}, u32[]{:S(2)}, u32[]{:S(2)}) collective-permute-start(bf16[2,3,32,640]{3,2,0,1:T(8,128)(2,1)S(1)} %pad_maximum_fusion.4), channel_id=1, source_target_pairs={{12,0},{0,4},{4,8},{8,12},{13,1},{1,5},{5,9},{9,13},{14,2},{2,6},{... | collective-permute-start | bytes 737288 | tf_op jit(solution)/shard_map/ppermute | solution.py:378
  15.1 0.1 copy.118
  15.3 0.2 mul.30
  15.5 0.2 copy.117
  15.8 0.2 fusion.2.refs_4_.refs_5_
  16.0 4.8 %collective-permute-done.2 = bf16[2,3,32,640]{3,2,0,1:T(8,128)(2,1)S(1)} collective-permute-done((bf16[2,3,32,640]{3,2,0,1:T(8,128)(2,1)S(1)}, bf16[2,3,32,640]{3,2,0,1:T(8,128)(2,1)S(1)}, u32[]{:S(2)}, u32[]{:S(2)}) %collective-permute-start.2) | collective-permute-done | bytes 245792 | tf_op jit(solution)/shard_map/ppermute | solution.py:378
  21.0 1.3 %collective-permute-done.3 = bf16[2,3,32,640]{3,2,0,1:T(8,128)(2,1)S(1)} collective-permute-done((bf16[2,3,32,640]{3,2,0,1:T(8,128)(2,1)S(1)}, bf16[2,3,32,640]{3,2,0,1:T(8,128)(2,1)S(1)}, u32[]{:S(2)}, u32[]{:S(2)}) %collective-permute-start.3) | collective-permute-done | bytes 245792 | tf_op jit(solution)/shard_map/ppermute | solution.py:378
  22.2 0.1 pad_maximum_fusion.1
  22.3 3.3 %collective-permute-start.5 = (bf16[3,3,32,640]{3,2,0,1:T(8,128)(2,1)S(1)}, bf16[3,3,32,640]{3,2,0,1:T(8,128)(2,1)S(1)}, u32[]{:S(2)}, u32[]{:S(2)}) collective-permute-start(bf16[3,3,32,640]{3,2,0,1:T(8,128)(2,1)S(1)} %pad_maximum_fusion.1), channel_id=1, source_target_pairs={{16,0},{32,16},{48,32},{64,48},{80,64},{96,80},{112,96},{0,112},{1... | collective-permute-start | bytes 1105928 | tf_op jit(solution)/shard_map/ppermute | solution.py:378
  25.6 0.1 pad_maximum_fusion
  25.6 0.1 collective-permute-start.4
  25.8 6.5 %own_part_0.1 = (f32[72,512]{1,0:T(8,128)S(1)}, f32[8,72,640]{2,1,0:T(8,128)S(1)}, f32[4,72,640]{2,1,0:T(8,128)S(1)}, bf16[640,576]{1,0:T(8,128)(2,1)S(1)}, s32[2]{0:T(128)S(1)}) custom-call(s32[2]{0:T(128)S(1)} %bitcast.46, bf16[2,3,32,640]{3,2,1,0:T(8,128)(2,1)S(1)} %copy.119.refs_1_, bf16[2,3,32,640]{3,2,1,0:T(8,128)(2,1)S(1)} %copy.120.refs_2_, ...), custom_call_target="tpu_custom_call" | custom-call | flops 6039797760 | bytes 4000000 | tf_op jit(solution)/shard_map/own_part_0/pallas_call | solution.py:335
  32.3 0.9 copy-done.12
  33.2 0.3 collective-permute-done.5
  33.5 4.5 %collective-permute-done.4 = bf16[3,3,32,640]{3,2,0,1:T(8,128)(2,1)S(1)} collective-permute-done((bf16[3,3,32,640]{3,2,0,1:T(8,128)(2,1)S(1)}, bf16[3,3,32,640]{3,2,0,1:T(8,128)(2,1)S(1)}, u32[]{:S(2)}, u32[]{:S(2)}) %collective-permute-start.4) | collective-permute-done | bytes 368672 | tf_op jit(solution)/shard_map/ppermute | solution.py:378
  38.0 5.7 %side_part_0.1 = (bf16[64,512]{1,0:T(8,128)(2,1)S(1)}, f32[8,72,384]{2,1,0:T(8,128)S(1)}, f32[4,72,384]{2,1,0:T(8,128)S(1)}, bf16[2,384,288]{2,1,0:T(8,128)(2,1)S(1)}, s32[2]{0:T(128)S(1)}) custom-call(s32[2]{0:T(128)S(1)} %bitcast.47, bf16[3,3,32,640]{3,2,1,0:T(8,128)(2,1)S(1)} %copy.122.refs_1_, bf16[3,3,32,640]{3,2,1,0:T(8,128)(2,1)S(1)} %copy.123.refs_2_, ...), custom_call_target="tpu_custom_call" | custom-call | flops 3019898880 | bytes 4000000 | tf_op jit(solution)/shard_map/side_part_0/pallas_call | solution.py:364
  43.7 0.8 collective-permute-start.6
  44.5 2.0 %collective-permute-start.7 = (bf16[2,32,512]{2,1,0:T(8,128)(2,1)S(1)}, bf16[2,32,512]{2,1,0:T(8,128)(2,1)S(1)}, u32[]{:S(2)}, u32[]{:S(2)}) collective-permute-start(bf16[2,32,512]{2,1,0:T(8,128)(2,1)S(1)} %bitcast.42), channel_id=1, source_target_pairs={{1,0},{2,1},{3,2},{0,3},{5,4},{6,5},{7,6},{4,7},{9,8},{10,9},{11,1... | collective-permute-start | bytes 196616 | tf_op jit(solution)/shard_map/ppermute | solution.py:378
  46.5 0.1 copy.129.refs_10_
  46.6 2.2 %collective-permute-done.6 = bf16[2,32,512]{2,1,0:T(8,128)(2,1)S(1)} collective-permute-done((bf16[2,32,512]{2,1,0:T(8,128)(2,1)S(1)}, bf16[2,32,512]{2,1,0:T(8,128)(2,1)S(1)}, u32[]{:S(2)}, u32[]{:S(2)}) %collective-permute-start.6) | collective-permute-done | bytes 65568 | tf_op jit(solution)/shard_map/ppermute | solution.py:378
  48.8 3.7 %collective-permute-start.8 = (bf16[2,3,32,512]{3,2,0,1:T(8,128)(2,1)S(1)}, bf16[2,3,32,512]{3,2,0,1:T(8,128)(2,1)S(1)}, u32[]{:S(2)}, u32[]{:S(2)}) collective-permute-start(bf16[2,3,32,512]{3,2,0,1:T(8,128)(2,1)S(1)} %pad_maximum_fusion.5), channel_id=1, source_target_pairs={{12,0},{0,4},{4,8},{8,12},{13,1},{1,5},{5,9},{9,13},{14,2},{2,6},{... | collective-permute-start | bytes 589832 | tf_op jit(solution)/shard_map/ppermute | solution.py:378
  52.6 4.2 %collective-permute-done.8 = bf16[2,3,32,512]{3,2,0,1:T(8,128)(2,1)S(1)} collective-permute-done((bf16[2,3,32,512]{3,2,0,1:T(8,128)(2,1)S(1)}, bf16[2,3,32,512]{3,2,0,1:T(8,128)(2,1)S(1)}, u32[]{:S(2)}, u32[]{:S(2)}) %collective-permute-start.8) | collective-permute-done | bytes 196640 | tf_op jit(solution)/shard_map/ppermute | solution.py:378
  56.8 2.3 %collective-permute-done.9 = bf16[2,3,32,512]{3,2,0,1:T(8,128)(2,1)S(1)} collective-permute-done((bf16[2,3,32,512]{3,2,0,1:T(8,128)(2,1)S(1)}, bf16[2,3,32,512]{3,2,0,1:T(8,128)(2,1)S(1)}, u32[]{:S(2)}, u32[]{:S(2)}) %collective-permute-start.9) | collective-permute-done | bytes 196640 | tf_op jit(solution)/shard_map/ppermute | solution.py:378
  59.2 6.7 %collective-permute-start.11 = (bf16[3,3,32,512]{3,2,0,1:T(8,128)(2,1)S(1)}, bf16[3,3,32,512]{3,2,0,1:T(8,128)(2,1)S(1)}, u32[]{:S(2)}, u32[]{:S(2)}) collective-permute-start(bf16[3,3,32,512]{3,2,0,1:T(8,128)(2,1)S(1)} %pad_maximum_fusion.3), channel_id=1, source_target_pairs={{16,0},{32,16},{48,32},{64,48},{80,64},{96,80},{112,96},{0,112},{1... | collective-permute-start | bytes 884744 | tf_op jit(solution)/shard_map/ppermute | solution.py:378
  66.0 0.1 collective-permute-start.10
  66.1 4.0 %own_part_1.1.refs_4_ = f32[72,512]{1,0:T(8,128)S(1)} custom-call(s32[2]{0:T(128)S(1)} %bitcast.48, bf16[2,3,32,512]{3,2,1,0:T(8,128)(2,1)S(1)} %copy.124.refs_1_, bf16[2,3,32,512]{3,2,1,0:T(8,128)(2,1)S(1)} %copy.125.refs_2_, bf16[2,3,32,512]{3,2,1,0:T(8,128)(2,1)S(1)} %copy.126.refs_3_, bf16[2,512,80]{2,1,0:T(8,128)(2,1)S(1)} %fusion.2.refs_4_.refs_5_, ...), custom_call_target="tpu_custom_call" | custom-call | flops 6039797760 | bytes 4000000 | tf_op jit(solution)/shard_map/own_part_1/pallas_call | solution.py:335
  70.1 1.6 %collective-permute-done.11 = bf16[3,3,32,512]{3,2,0,1:T(8,128)(2,1)S(1)} collective-permute-done((bf16[3,3,32,512]{3,2,0,1:T(8,128)(2,1)S(1)}, bf16[3,3,32,512]{3,2,0,1:T(8,128)(2,1)S(1)}, u32[]{:S(2)}, u32[]{:S(2)}) %collective-permute-start.11) | collective-permute-done | bytes 294944 | tf_op jit(solution)/shard_map/ppermute | solution.py:378
  71.7 4.4 %collective-permute-done.10 = bf16[3,3,32,512]{3,2,0,1:T(8,128)(2,1)S(1)} collective-permute-done((bf16[3,3,32,512]{3,2,0,1:T(8,128)(2,1)S(1)}, bf16[3,3,32,512]{3,2,0,1:T(8,128)(2,1)S(1)}, u32[]{:S(2)}, u32[]{:S(2)}) %collective-permute-start.10) | collective-permute-done | bytes 294944 | tf_op jit(solution)/shard_map/ppermute | solution.py:378
  76.2 4.5 %side_part_1.1 = (bf16[64,512]{1,0:T(8,128)(2,1)S(1)}, f32[128,128]{1,0:T(8,128)}) custom-call(s32[2]{0:T(128)S(1)} %bitcast.49, bf16[3,3,32,512]{3,2,1,0:T(8,128)(2,1)S(1)} %copy.127.refs_1_, bf16[3,3,32,512]{3,2,1,0:T(8,128)(2,1)S(1)} %copy.128.refs_2_, bf16[2,32,512]{2,1,0:T(8,128)(2,1)S(1)} %bitcast.44, f32[72,512]{1,0:T(8,128)S(1)} %own_part_1.1.refs_4_, ...), custom_call_target="tpu_custom_call" | custom-call | flops 3019898880 | bytes 4000000 | tf_op jit(solution)/shard_map/side_part_1/pallas_call | solution.py:364
  80.6 13.1 %all-to-all-start = ((f32[128,1,128]{2,1,0:T(1,128)}), f32[128,1,128]{2,1,0:T(1,128)S(1)}, u32[]{:S(2)}, u32[]{:S(2)}) async-start(f32[128,1,128]{2,1,0:T(1,128)} %bitcast.20), calls=%async_computation | async-start | bytes 131072 | tf_op jit(solution)/shard_map/all_to_all | solution.py:460
  93.7 0.6 slice.57
  94.4 0.6 copy.132
  95.0 8.4 %all-to-all-done = f32[128,1,128]{2,1,0:T(1,128)S(1)} async-done(((f32[128,1,128]{2,1,0:T(1,128)}), f32[128,1,128]{2,1,0:T(1,128)S(1)}, u32[]{:S(2)}, u32[]{:S(2)}) %all-to-all-start) | async-done | bytes 65568 | tf_op jit(solution)/shard_map/all_to_all | solution.py:460
  103.4 0.7 reduce_sum.9
  (65 shorter events, 0.8 us)
Async XLA Ops:
  0.6 14.6 %copy-start.15 = (bf16[2,8,64]{2,1,0:T(8,128)(2,1)S(1)}, bf16[2,8,64]{2,1,0:T(8,128)(2,1)}, u32[]{:S(2)}) copy-start(bf16[2,8,64]{2,1,0:T(8,128)(2,1)} %param.19) | copy-start | bytes 6148
  0.6 14.5 %copy-start.16 = (f32[2,64]{1,0:T(2,128)S(1)}, f32[2,64]{1,0:T(2,128)}, u32[]{:S(2)}) copy-start(f32[2,64]{1,0:T(2,128)} %param.20) | copy-start | bytes 1540
  4.0 5.2 %collective-permute-start = (bf16[2,32,640]{2,1,0:T(8,128)(2,1)S(1)}, bf16[2,32,640]{2,1,0:T(8,128)(2,1)S(1)}, u32[]{:S(2)}, u32[]{:S(2)}) collective-permute-start(bf16[2,32,640]{2,1,0:T(8,128)(2,1)S(1)} %get-tuple-element.64.refs_3_), channel_id=1, source_target_pairs={{3,0},{0,1},{1,2},{2,3},{7,4},{4,5},{5,6},{6,7},{11,8},{8,9},{9,10... | collective-permute-start | bytes 245768 | tf_op jit(solution)/shard_map/ppermute | solution.py:378
  6.1 3.3 %collective-permute-start.1 = (bf16[2,32,640]{2,1,0:T(8,128)(2,1)S(1)}, bf16[2,32,640]{2,1,0:T(8,128)(2,1)S(1)}, u32[]{:S(2)}, u32[]{:S(2)}) collective-permute-start(bf16[2,32,640]{2,1,0:T(8,128)(2,1)S(1)} %get-tuple-element.64.refs_3_), channel_id=1, source_target_pairs={{1,0},{2,1},{3,2},{0,3},{5,4},{6,5},{7,6},{4,7},{9,8},{10,9},{11,1... | collective-permute-start | bytes 245768 | tf_op jit(solution)/shard_map/ppermute | solution.py:378
  9.4 11.4 %collective-permute-start.2 = (bf16[2,3,32,640]{3,2,0,1:T(8,128)(2,1)S(1)}, bf16[2,3,32,640]{3,2,0,1:T(8,128)(2,1)S(1)}, u32[]{:S(2)}, u32[]{:S(2)}) collective-permute-start(bf16[2,3,32,640]{3,2,0,1:T(8,128)(2,1)S(1)} %pad_maximum_fusion.4), channel_id=1, source_target_pairs={{12,0},{0,4},{4,8},{8,12},{13,1},{1,5},{5,9},{9,13},{14,2},{2,6},{... | collective-permute-start | bytes 737288 | tf_op jit(solution)/shard_map/ppermute | solution.py:378
  15.1 7.1 %collective-permute-start.3 = (bf16[2,3,32,640]{3,2,0,1:T(8,128)(2,1)S(1)}, bf16[2,3,32,640]{3,2,0,1:T(8,128)(2,1)S(1)}, u32[]{:S(2)}, u32[]{:S(2)}) collective-permute-start(bf16[2,3,32,640]{3,2,0,1:T(8,128)(2,1)S(1)} %pad_maximum_fusion.4), channel_id=1, source_target_pairs={{4,0},{8,4},{12,8},{0,12},{5,1},{9,5},{13,9},{1,13},{6,2},{10,6},{... | collective-permute-start | bytes 737288 | tf_op jit(solution)/shard_map/ppermute | solution.py:378
  20.9 4.9 %copy-start = (s32[2,1,1]{0,2,1:T(1,128)S(1)}, s32[2,1,1]{0,2,1:T(1,128)}, u32[]{:S(2)}) copy-start(s32[2,1,1]{0,2,1:T(1,128)} %param.16) | copy-start | bytes 28
  20.9 4.9 %copy-start.1 = (bf16[2,128,512]{2,1,0:T(8,128)(2,1)S(1)}, bf16[2,128,512]{2,1,0:T(8,128)(2,1)}, u32[]{:S(2)}) copy-start(bf16[2,128,512]{2,1,0:T(8,128)(2,1)} %refs_9_.4) | copy-start | bytes 786436
  20.9 4.9 %copy-start.2 = (bf16[2,64,512]{2,1,0:T(8,128)(2,1)S(1)}, bf16[2,64,512]{2,1,0:T(8,128)(2,1)}, u32[]{:S(2)}) copy-start(bf16[2,64,512]{2,1,0:T(8,128)(2,1)} %refs_6_.7) | copy-start | bytes 393220
  20.9 4.9 %copy-start.3 = (bf16[2,128,128]{2,1,0:T(8,128)(2,1)S(1)}, bf16[2,128,128]{2,1,0:T(8,128)(2,1)}, u32[]{:S(2)}) copy-start(bf16[2,128,128]{2,1,0:T(8,128)(2,1)} %refs_7_.7) | copy-start | bytes 196612
  20.9 4.9 %copy-start.4 = (f32[2,128]{1,0:T(2,128)S(1)}, f32[2,128]{1,0:T(2,128)}, u32[]{:S(2)}) copy-start(f32[2,128]{1,0:T(2,128)} %refs_8_.7) | copy-start | bytes 3076
  21.0 4.9 %copy-start.6 = (bf16[576,128]{1,0:T(8,128)(2,1)S(1)}, bf16[576,128]{1,0:T(8,128)(2,1)}, u32[]{:S(2)}) copy-start(bf16[576,128]{1,0:T(8,128)(2,1)} %constant.14.clone.refs_9_) | copy-start | bytes 442372
  22.3 11.2 %collective-permute-start.5 = (bf16[3,3,32,640]{3,2,0,1:T(8,128)(2,1)S(1)}, bf16[3,3,32,640]{3,2,0,1:T(8,128)(2,1)S(1)}, u32[]{:S(2)}, u32[]{:S(2)}) collective-permute-start(bf16[3,3,32,640]{3,2,0,1:T(8,128)(2,1)S(1)} %pad_maximum_fusion.1), channel_id=1, source_target_pairs={{16,0},{32,16},{48,32},{64,48},{80,64},{96,80},{112,96},{0,112},{1... | collective-permute-start | bytes 1105928 | tf_op jit(solution)/shard_map/ppermute | solution.py:378
  25.6 12.3 %collective-permute-start.4 = (bf16[3,3,32,640]{3,2,0,1:T(8,128)(2,1)S(1)}, bf16[3,3,32,640]{3,2,0,1:T(8,128)(2,1)S(1)}, u32[]{:S(2)}, u32[]{:S(2)}) collective-permute-start(bf16[3,3,32,640]{3,2,0,1:T(8,128)(2,1)S(1)} %pad_maximum_fusion), channel_id=1, source_target_pairs={{112,0},{0,16},{16,32},{32,48},{48,64},{64,80},{80,96},{96,112},{1... | collective-permute-start | bytes 1105928 | tf_op jit(solution)/shard_map/ppermute | solution.py:378
  32.3 0.9 copy-start.12
  33.2 10.5 %copy-start.8 = (f32[8,72,640]{2,1,0:T(8,128)}, f32[8,72,640]{2,1,0:T(8,128)S(1)}, u32[]{:S(2)}) copy-start(f32[8,72,640]{2,1,0:T(8,128)S(1)} %get-tuple-element.23.refs_9_) | copy-start | bytes 4423684
  33.2 10.5 %copy-start.10 = (bf16[640,576]{1,0:T(8,128)(2,1)}, bf16[640,576]{1,0:T(8,128)(2,1)S(1)}, u32[]{:S(2)}) copy-start(bf16[640,576]{1,0:T(8,128)(2,1)S(1)} %get-tuple-element.25.refs_11_) | copy-start | bytes 2211844
  33.2 4.8 %copy-start.7 = (bf16[288,128]{1,0:T(8,128)(2,1)S(1)}, bf16[288,128]{1,0:T(8,128)(2,1)}, u32[]{:S(2)}) copy-start(bf16[288,128]{1,0:T(8,128)(2,1)} %constant.15.clone.refs_10_) | copy-start | bytes 221188
  38.0 8.4 %copy-start.14 = (bf16[128,64]{0,1:T(8,128)(2,1)S(1)}, bf16[128,64]{0,1:T(8,128)(2,1)}, u32[]{:S(2)}) copy-start(bf16[128,64]{0,1:T(8,128)(2,1)} %param.25) | copy-start | bytes 49156
  43.7 5.1 %collective-permute-start.6 = (bf16[2,32,512]{2,1,0:T(8,128)(2,1)S(1)}, bf16[2,32,512]{2,1,0:T(8,128)(2,1)S(1)}, u32[]{:S(2)}, u32[]{:S(2)}) collective-permute-start(bf16[2,32,512]{2,1,0:T(8,128)(2,1)S(1)} %bitcast.41), channel_id=1, source_target_pairs={{3,0},{0,1},{1,2},{2,3},{7,4},{4,5},{5,6},{6,7},{11,8},{8,9},{9,10... | collective-permute-start | bytes 196616 | tf_op jit(solution)/shard_map/ppermute | solution.py:378
  44.5 4.3 %collective-permute-start.7 = (bf16[2,32,512]{2,1,0:T(8,128)(2,1)S(1)}, bf16[2,32,512]{2,1,0:T(8,128)(2,1)S(1)}, u32[]{:S(2)}, u32[]{:S(2)}) collective-permute-start(bf16[2,32,512]{2,1,0:T(8,128)(2,1)S(1)} %bitcast.42), channel_id=1, source_target_pairs={{1,0},{2,1},{3,2},{0,3},{5,4},{6,5},{7,6},{4,7},{9,8},{10,9},{11,1... | collective-permute-start | bytes 196616 | tf_op jit(solution)/shard_map/ppermute | solution.py:378
  48.8 8.0 %collective-permute-start.8 = (bf16[2,3,32,512]{3,2,0,1:T(8,128)(2,1)S(1)}, bf16[2,3,32,512]{3,2,0,1:T(8,128)(2,1)S(1)}, u32[]{:S(2)}, u32[]{:S(2)}) collective-permute-start(bf16[2,3,32,512]{3,2,0,1:T(8,128)(2,1)S(1)} %pad_maximum_fusion.5), channel_id=1, source_target_pairs={{12,0},{0,4},{4,8},{8,12},{13,1},{1,5},{5,9},{9,13},{14,2},{2,6},{... | collective-permute-start | bytes 589832 | tf_op jit(solution)/shard_map/ppermute | solution.py:378
  52.5 6.6 %collective-permute-start.9 = (bf16[2,3,32,512]{3,2,0,1:T(8,128)(2,1)S(1)}, bf16[2,3,32,512]{3,2,0,1:T(8,128)(2,1)S(1)}, u32[]{:S(2)}, u32[]{:S(2)}) collective-permute-start(bf16[2,3,32,512]{3,2,0,1:T(8,128)(2,1)S(1)} %pad_maximum_fusion.5), channel_id=1, source_target_pairs={{4,0},{8,4},{12,8},{0,12},{5,1},{9,5},{13,9},{1,13},{6,2},{10,6},{... | collective-permute-start | bytes 589832 | tf_op jit(solution)/shard_map/ppermute | solution.py:378
  52.5 13.6 %copy-start.13 = (f32[4,72,640]{2,1,0:T(8,128)S(1)}, f32[4,72,640]{2,1,0:T(8,128)}, u32[]{:S(2)}) copy-start(f32[4,72,640]{2,1,0:T(8,128)} %copy-done.12) | copy-start | bytes 2211844
  52.6 13.5 %copy-start.9 = (f32[8,72,640]{2,1,0:T(8,128)S(1)}, f32[8,72,640]{2,1,0:T(8,128)}, u32[]{:S(2)}) copy-start(f32[8,72,640]{2,1,0:T(8,128)} %copy-done.8) | copy-start | bytes 4423684
  52.6 13.5 %copy-start.11 = (bf16[640,576]{1,0:T(8,128)(2,1)S(1)}, bf16[640,576]{1,0:T(8,128)(2,1)}, u32[]{:S(2)}) copy-start(bf16[640,576]{1,0:T(8,128)(2,1)} %copy-done.10) | copy-start | bytes 2211844
  59.2 12.6 %collective-permute-start.11 = (bf16[3,3,32,512]{3,2,0,1:T(8,128)(2,1)S(1)}, bf16[3,3,32,512]{3,2,0,1:T(8,128)(2,1)S(1)}, u32[]{:S(2)}, u32[]{:S(2)}) collective-permute-start(bf16[3,3,32,512]{3,2,0,1:T(8,128)(2,1)S(1)} %pad_maximum_fusion.3), channel_id=1, source_target_pairs={{16,0},{32,16},{48,32},{64,48},{80,64},{96,80},{112,96},{0,112},{1... | collective-permute-start | bytes 884744 | tf_op jit(solution)/shard_map/ppermute | solution.py:378
  66.0 10.2 %collective-permute-start.10 = (bf16[3,3,32,512]{3,2,0,1:T(8,128)(2,1)S(1)}, bf16[3,3,32,512]{3,2,0,1:T(8,128)(2,1)S(1)}, u32[]{:S(2)}, u32[]{:S(2)}) collective-permute-start(bf16[3,3,32,512]{3,2,0,1:T(8,128)(2,1)S(1)} %pad_maximum_fusion.2), channel_id=1, source_target_pairs={{112,0},{0,16},{16,32},{32,48},{48,64},{64,80},{80,96},{96,112},{1... | collective-permute-start | bytes 884744 | tf_op jit(solution)/shard_map/ppermute | solution.py:378
  66.1 10.0 %copy-start.5 = (f32[64]{0:T(128)S(1)}, f32[64]{0:T(128)}, u32[]{:S(2)}) copy-start(f32[64]{0:T(128)} %param.26) | copy-start | bytes 772
  80.6 22.8 %all-to-all-start = ((f32[128,1,128]{2,1,0:T(1,128)}), f32[128,1,128]{2,1,0:T(1,128)S(1)}, u32[]{:S(2)}, u32[]{:S(2)}) async-start(f32[128,1,128]{2,1,0:T(1,128)} %bitcast.20), calls=%async_computation | async-start | bytes 131072 | tf_op jit(solution)/shard_map/all_to_all | solution.py:460
